TPU v7x, 32 devices: a whole 2x2x4 slice. The times are simulated.
32 devices in a mesh: seq: 8 (over z, y), batch: 4 (over x, core).
Axes of the slice: x: 2, y: 2, z: 4, core: 2. Of those that a mesh axis runs over, the one named last changes fastest.
Arguments:
- incoming_symbols: bfloat16 [8, 2048, 1024], P('batch', 'seq'), may hold values from -6 to 6
- article_sizes: int32 [8, 8], P('batch'), may hold values from 1 to 2041, as said below
- mixer_norm_scale: float32 [1024], replicated, may hold values from 0.1 to 1.9
- mixer_norm_offset: float32 [1024], replicated, may hold values from -2 to 2
- temporal_lookup_share: float32 [1024], replicated, may hold values from 0 to 1
- temporal_payload_share: float32 [1024], replicated, may hold values from 0 to 1
- temporal_gate_share: float32 [1024], replicated, may hold values from 0 to 1
- fading_log_rates: float32 [1024], replicated
- present_reward_vector: float32 [1024], replicated, may hold values from -1 to 1
- lookup_matrix: bfloat16 [1024, 1024], replicated, may hold values from -0.1875 to 0.1875
- payload_matrix: bfloat16 [1024, 1024], replicated, may hold values from -0.1875 to 0.1875
- gate_matrix: bfloat16 [1024, 1024], replicated, may hold values from -0.1875 to 0.1875
- emission_matrix: bfloat16 [1024, 1024], replicated, may hold values from -1.5 to 1.5
- channel_norm_scale: float32 [1024], replicated, may hold values from 0.1 to 1.9
- channel_norm_offset: float32 [1024], replicated, may hold values from -2 to 2
- channel_lookup_share: float32 [1024], replicated, may hold values from 0 to 1
- channel_gate_share: float32 [1024], replicated, may hold values from 0 to 1
- channel_lookup_matrix: bfloat16 [1024, 4096], replicated, may hold values from -0.1875 to 0.1875
- channel_payload_matrix: bfloat16 [4096, 1024], replicated, may hold values from -0.09375 to 0.09375
- channel_gate_matrix: bfloat16 [1024, 1024], replicated, may hold values from -0.1875 to 0.1875
- final_cotangent: bfloat16 [8, 2048, 1024], P('batch', 'seq'), may hold values from -6 to 6
Outputs:
- layer_out: bfloat16 [8, 2048, 1024], P('batch', 'seq')
- grad_tokens: bfloat16 [8, 2048, 1024], P('batch', 'seq')
- grad_att_ln_gain: float32 [1024], P('seq')
- grad_att_ln_bias: float32 [1024], P('seq')
- grad_mix_key: float32 [1024], P('seq')
- grad_mix_value: float32 [1024], P('seq')
- grad_mix_recep: float32 [1024], P('seq')
- grad_time_decay: float32 [1024], P('seq')
- reward_slope_array: float32 [1024], P('seq')
- grad_key_weight: float32 [1024, 1024], P('seq')
- grad_value_weight: float32 [1024, 1024], P('seq')
- grad_recep_weight: float32 [1024, 1024], P('seq')
- grad_output_weight: float32 [1024, 1024], P('seq')
- grad_ffn_ln_gain: float32 [1024], P('seq')
- grad_ffn_ln_bias: float32 [1024], P('seq')
- grad_ffn_mix_key: float32 [1024], P('seq')
- grad_ffn_mix_recep: float32 [1024], P('seq')
- grad_ffn_key_weight: float32 [1024, 4096], P('seq')
- grad_ffn_value_weight: float32 [4096, 1024], P('seq')
- grad_ffn_recep_weight: float32 [1024, 1024], P('seq')
Inputs may be any that keep to these rules, and one draw needn't show every extreme that they name: `article_sizes`: each row's lengths sum to 2048. In each row one document, whose place in the row is drawn from the seed, is longer than 1792; every other one has at most 32 positions. In one row, drawn from the seed, every other document has exactly one position.
All inputs are finite; a program needn't handle non-finite values.
Results may differ from a plain program's by a relative error of at most 0.009.
Values sent between devices are 32-bit elements; how exact they have to be, the bound alone decides.
No kernel may reach another device: no remote copies, remote signals or barrier semaphores. Data moves between devices by JAX's collectives and lax.ppermute only.
A program may use at most 192 MiB of HBM per device.

v0:
```python
import jax
import jax.numpy as jnp
from jax import lax
from jax.sharding import PartitionSpec as P


def shifted(block, axis, distance):
    devices = range(lax.axis_size(axis))
    route = [(i - distance, i) for i in devices if i - distance in devices]
    return lax.ppermute(block, axis, route)


def entering_2(value, axis, join, neutral, backward):
    count, mine = (lax.axis_size(axis), lax.axis_index(axis))
    pieces = jax.tree.map(lambda part: lax.all_gather(part, axis), value)
    if backward:
        pieces = jax.tree.map(lambda part: part[::-1], pieces)
        mine = count - 1 - mine
    running = jax.tree.map(
        lambda part, zero: jnp.full_like(part, 0) + jnp.asarray(zero, part.dtype), value, neutral
    )

    def lap(position, running):
        longer = join(running, jax.tree.map(lambda part: part[position], pieces))
        return jax.tree.map(lambda new, old: jnp.where(position < mine, new, old), longer, running)

    return lax.fori_loop(0, count - 1, lap, running)


def norm_rows(value_rows, gain_vec, bias_vec):
    row_mean = jnp.mean(value_rows, axis=-1, keepdims=True)
    centred = value_rows - row_mean
    inv_std = lax.rsqrt(jnp.mean(centred * centred, axis=-1, keepdims=True) + 1e-05)
    normed = centred * inv_std
    return (normed * gain_vec + bias_vec, normed, inv_std)


def norm_back(grad_in, normed, inv_std, gain_vec):
    scaled = grad_in * gain_vec
    return inv_std * (
        scaled
        - jnp.mean(scaled, axis=-1, keepdims=True)
        - normed * jnp.mean(scaled * normed, axis=-1, keepdims=True)
    )


def project(left_side, right_side):
    return jnp.einsum("rcd,de->rce", left_side, right_side, preferred_element_type=jnp.float32)


def project_back(grad_in, right_side):
    return jnp.einsum("rce,de->rcd", grad_in, right_side, preferred_element_type=jnp.float32)


def weight_grad(left_side, grad_in):
    return jnp.einsum("rcd,rce->de", left_side, grad_in, preferred_element_type=jnp.float32)


def with_previous(value_rows, edge_row, retain_flags):
    earlier = jnp.concatenate([edge_row[:, None, :], value_rows[:, :-1, :]], axis=1)
    return earlier * retain_flags[:, :, None]


def chain_states(earlier_part, later_part):
    return (
        later_part[2] * earlier_part[0] + later_part[0],
        later_part[2] * earlier_part[1] + later_part[1],
        earlier_part[2] * later_part[2],
    )


def block_prefix(inputs, resets, decay_rate):
    rows_here, group_len, feature_count = inputs[0].shape
    block_len = 16
    blocks = group_len // block_len
    block_resets = resets.reshape(rows_here, blocks, block_len)
    segment = jnp.cumsum(block_resets, axis=2)
    offsets = jnp.arange(block_len, dtype=jnp.float32)
    step_lag = offsets[:, None] - offsets[None, :] - 1.0
    decay_pow = jnp.exp(-jnp.maximum(step_lag, 0.0)[:, :, None] * decay_rate)
    same_seg = jnp.where(
        (segment[:, :, :, None] == segment[:, :, None, :]) & (step_lag >= 0.0), 1.0, 0.0
    )
    weights = same_seg[:, :, :, :, None] * decay_pow
    tail_pow = jnp.exp(-(block_len - 1.0 - offsets)[:, None] * decay_rate)
    tail_mask = jnp.where(segment == segment[:, :, -1:], 1.0, 0.0)[:, :, :, None] * tail_pow
    clear_mask = jnp.where(segment == 0.0, 1.0, 0.0)
    block_gain = clear_mask[:, :, -1:] * jnp.exp(-block_len * decay_rate)
    lead_pow = jnp.exp(-offsets[:, None] * decay_rate)
    shaped = [member.reshape(rows_here, blocks, block_len, feature_count) for member in inputs]
    inner_sums = [
        jnp.einsum("rbtsd,rbsd->rbtd", weights, member, precision=lax.Precision.HIGHEST)
        for member in shaped
    ]
    tail_sums = [jnp.sum(tail_mask * member, axis=2) for member in shaped]

    def advance(accumulated_pair, block_piece):
        gain_piece = block_piece[0]
        updated = tuple(
            (
                gain_piece * running_part + tail_part
                for running_part, tail_part in zip(accumulated_pair, block_piece[1:])
            )
        )
        return (updated, accumulated_pair)

    zero_state = jnp.zeros((rows_here, feature_count), jnp.float32)
    finals, entering = lax.scan(
        advance,
        tuple((zero_state for member in shaped)),
        tuple((jnp.swapaxes(part_sum, 0, 1) for part_sum in [block_gain] + tail_sums)),
    )
    states = []
    for inner_sum, entered in zip(inner_sums, entering):
        carried = clear_mask[:, :, :, None] * lead_pow * jnp.swapaxes(entered, 0, 1)[:, :, None, :]
        states.append((inner_sum + carried).reshape(rows_here, group_len, feature_count))
    group_gain = jnp.where(jnp.sum(resets, axis=1, keepdims=True) == 0.0, 1.0, 0.0) * jnp.exp(
        -group_len * decay_rate
    )
    return (states, finals, group_gain)


def attach(states, entering, resets, decay_rate):
    group_len = resets.shape[1]
    clear_mask = jnp.where(jnp.cumsum(resets, axis=1) == 0.0, 1.0, 0.0)[:, :, None]
    lead_pow = jnp.exp(-jnp.arange(group_len, dtype=jnp.float32)[:, None] * decay_rate)
    return [
        local_part + clear_mask * lead_pow * incoming[:, None, :]
        for local_part, incoming in zip(states, entering)
    ]


def shards(
    incoming_symbols,
    article_sizes,
    mixer_norm_scale,
    mixer_norm_offset,
    temporal_lookup_share,
    temporal_payload_share,
    temporal_gate_share,
    fading_log_rates,
    present_reward_vector,
    lookup_matrix,
    payload_matrix,
    gate_matrix,
    emission_matrix,
    channel_norm_scale,
    channel_norm_offset,
    channel_lookup_share,
    channel_gate_share,
    channel_lookup_matrix,
    channel_payload_matrix,
    channel_gate_matrix,
    final_cotangent,
):
    rows_here, group_len, feature_count = incoming_symbols.shape
    doc_ends = jnp.cumsum(article_sizes, axis=1)
    begins = doc_ends - article_sizes
    position = lax.axis_index("seq") * group_len + jnp.arange(group_len, dtype=jnp.int32)
    starts = jnp.where(
        jnp.any(position[None, :, None] == begins[:, None, :], axis=2), 1.0, 0.0
    ).astype(jnp.float32)
    retain_flags = 1.0 - starts
    symbol_entries = incoming_symbols.astype(jnp.float32)
    att_normed, att_unit, att_inv = norm_rows(symbol_entries, mixer_norm_scale, mixer_norm_offset)
    att_edge = shifted(att_normed[:, -1, :], "seq", 1)
    att_prev = with_previous(att_normed, att_edge, retain_flags)
    key_mixed = (
        att_normed * temporal_lookup_share + att_prev * (1.0 - temporal_lookup_share)
    ).astype(jnp.bfloat16)
    value_mixed = (
        att_normed * temporal_payload_share + att_prev * (1.0 - temporal_payload_share)
    ).astype(jnp.bfloat16)
    recep_mixed = (
        att_normed * temporal_gate_share + att_prev * (1.0 - temporal_gate_share)
    ).astype(jnp.bfloat16)
    lookup_mapped = project(key_mixed, lookup_matrix)
    payload_mapped = project(value_mixed, payload_matrix)
    recep_proj = project(recep_mixed, gate_matrix)
    decay_rate = jnp.exp(fading_log_rates)
    power_lookup_arg = jnp.exp(lookup_mapped)
    local_states, local_tails, group_gain = block_prefix(
        (power_lookup_arg * payload_mapped, power_lookup_arg), starts, decay_rate
    )
    zero_state = jnp.zeros((rows_here, feature_count), jnp.float32)
    unit_gain = jnp.ones((rows_here, feature_count), jnp.float32)
    num_in, den_in, gain_in = entering_2(
        (local_tails[0], local_tails[1], group_gain),
        "seq",
        chain_states,
        (zero_state, zero_state, unit_gain),
        False,
    )
    upper_sum_memory, lower_sum_memory = attach(local_states, (num_in, den_in), starts, decay_rate)
    reward_power_arg = jnp.exp(present_reward_vector + lookup_mapped)
    scaled_lower_sum = lower_sum_memory + reward_power_arg
    scaled_lookup_payload = (
        upper_sum_memory + reward_power_arg * payload_mapped
    ) / scaled_lower_sum
    recep_sig = jax.nn.sigmoid(recep_proj)
    gated = (recep_sig * scaled_lookup_payload).astype(jnp.bfloat16)
    after_att = symbol_entries + project(gated, emission_matrix)
    ffn_normed, ffn_unit, ffn_inv = norm_rows(after_att, channel_norm_scale, channel_norm_offset)
    ffn_edge = shifted(ffn_normed[:, -1, :], "seq", 1)
    ffn_prev = with_previous(ffn_normed, ffn_edge, retain_flags)
    ffn_key_mixed = (
        ffn_normed * channel_lookup_share + ffn_prev * (1.0 - channel_lookup_share)
    ).astype(jnp.bfloat16)
    ffn_recep_mixed = (
        ffn_normed * channel_gate_share + ffn_prev * (1.0 - channel_gate_share)
    ).astype(jnp.bfloat16)
    hidden_pre = project(ffn_key_mixed, channel_lookup_matrix)
    squared = jnp.square(jnp.maximum(hidden_pre, 0.0)).astype(jnp.bfloat16)
    ffn_value = project(squared, channel_payload_matrix)
    ffn_gate = jax.nn.sigmoid(project(ffn_recep_mixed, channel_gate_matrix))
    layer_out = (after_att + ffn_gate * ffn_value).astype(jnp.bfloat16)
    grad_top = final_cotangent.astype(jnp.float32)
    grad_fvalue = (grad_top * ffn_gate).astype(jnp.bfloat16)
    grad_frecep = (grad_top * ffn_value * (ffn_gate * (1.0 - ffn_gate))).astype(jnp.bfloat16)
    grad_squared = project_back(grad_fvalue, channel_payload_matrix)
    grad_hidden = (grad_squared * (2.0 * jnp.maximum(hidden_pre, 0.0))).astype(jnp.bfloat16)
    grad_ffn_value_weight = weight_grad(squared, grad_fvalue)
    grad_ffn_recep_weight = weight_grad(ffn_recep_mixed, grad_frecep)
    grad_ffn_key_weight = weight_grad(ffn_key_mixed, grad_hidden)
    grad_fkey_in = project_back(grad_hidden, channel_lookup_matrix)
    grad_frecep_in = project_back(grad_frecep, channel_gate_matrix)
    ffn_delta = ffn_normed - ffn_prev
    grad_ffn_mix_key = jnp.sum(grad_fkey_in * ffn_delta, axis=(0, 1))
    grad_ffn_mix_recep = jnp.sum(grad_frecep_in * ffn_delta, axis=(0, 1))
    grad_ffn_prev = (
        grad_fkey_in * (1.0 - channel_lookup_share) + grad_frecep_in * (1.0 - channel_gate_share)
    ) * retain_flags[:, :, None]
    ffn_back_edge = shifted(grad_ffn_prev[:, 0, :], "seq", -1)
    grad_ffn_normed = (
        grad_fkey_in * channel_lookup_share
        + grad_frecep_in * channel_gate_share
        + jnp.concatenate([grad_ffn_prev[:, 1:, :], ffn_back_edge[:, None, :]], axis=1)
    )
    grad_ffn_ln_gain = jnp.sum(grad_ffn_normed * ffn_unit, axis=(0, 1))
    grad_ffn_ln_bias = jnp.sum(grad_ffn_normed, axis=(0, 1))
    grad_after = grad_top + norm_back(grad_ffn_normed, ffn_unit, ffn_inv, channel_norm_scale)
    grad_att_out = grad_after.astype(jnp.bfloat16)
    grad_output_weight = weight_grad(gated, grad_att_out)
    grad_gated = project_back(grad_att_out, emission_matrix)
    grad_wkv = grad_gated * recep_sig
    grad_recep = (grad_gated * scaled_lookup_payload * (recep_sig * (1.0 - recep_sig))).astype(
        jnp.bfloat16
    )
    upper_sum_slope = grad_wkv / scaled_lower_sum
    denominator_gradient = -grad_wkv * scaled_lookup_payload / scaled_lower_sum
    rev_resets = jnp.concatenate([jnp.zeros((rows_here, 1), jnp.float32), starts[:, :0:-1]], axis=1)
    back_states, back_tails, back_gain = block_prefix(
        (upper_sum_slope[:, ::-1, :], denominator_gradient[:, ::-1, :]), rev_resets, decay_rate
    )
    first_keep = retain_flags[:, :1]
    from_num, from_den, from_gain = entering_2(
        (back_tails[0] * first_keep, back_tails[1] * first_keep, back_gain * first_keep),
        "seq",
        chain_states,
        (zero_state, zero_state, unit_gain),
        True,
    )
    back_num, back_den = attach(back_states, (from_num, from_den), rev_resets, decay_rate)
    final_upper_sum = back_num[:, ::-1, :]
    trailing_denominator = back_den[:, ::-1, :]
    present_reward_piece = reward_power_arg * (
        upper_sum_slope * payload_mapped + denominator_gradient
    )
    value_gradient = (
        upper_sum_slope * reward_power_arg + final_upper_sum * power_lookup_arg
    ).astype(jnp.bfloat16)
    key_gradient = (
        present_reward_piece
        + power_lookup_arg * (final_upper_sum * payload_mapped + trailing_denominator)
    ).astype(jnp.bfloat16)
    reward_slope_array = jnp.sum(present_reward_piece, axis=(0, 1))
    grad_time_decay = (
        -decay_rate
        * jnp.exp(-decay_rate)
        * jnp.sum(
            upper_sum_memory * final_upper_sum + lower_sum_memory * trailing_denominator,
            axis=(0, 1),
        )
    )
    grad_key_weight = weight_grad(key_mixed, key_gradient)
    grad_value_weight = weight_grad(value_mixed, value_gradient)
    grad_recep_weight = weight_grad(recep_mixed, grad_recep)
    grad_key_in = project_back(key_gradient, lookup_matrix)
    grad_value_in = project_back(value_gradient, payload_matrix)
    grad_recep_in = project_back(grad_recep, gate_matrix)
    att_delta = att_normed - att_prev
    grad_mix_key = jnp.sum(grad_key_in * att_delta, axis=(0, 1))
    grad_mix_value = jnp.sum(grad_value_in * att_delta, axis=(0, 1))
    grad_mix_recep = jnp.sum(grad_recep_in * att_delta, axis=(0, 1))
    grad_att_prev = (
        grad_key_in * (1.0 - temporal_lookup_share)
        + grad_value_in * (1.0 - temporal_payload_share)
        + grad_recep_in * (1.0 - temporal_gate_share)
    ) * retain_flags[:, :, None]
    att_back_edge = shifted(grad_att_prev[:, 0, :], "seq", -1)
    grad_att_normed = (
        grad_key_in * temporal_lookup_share
        + grad_value_in * temporal_payload_share
        + grad_recep_in * temporal_gate_share
        + jnp.concatenate([grad_att_prev[:, 1:, :], att_back_edge[:, None, :]], axis=1)
    )
    grad_att_ln_gain = jnp.sum(grad_att_normed * att_unit, axis=(0, 1))
    grad_att_ln_bias = jnp.sum(grad_att_normed, axis=(0, 1))
    grad_tokens = (
        grad_after + norm_back(grad_att_normed, att_unit, att_inv, mixer_norm_scale)
    ).astype(jnp.bfloat16)
    shares = (
        lax.psum_scatter(grad_att_ln_gain, "seq", scatter_dimension=0, tiled=True),
        lax.psum_scatter(grad_att_ln_bias, "seq", scatter_dimension=0, tiled=True),
        lax.psum_scatter(grad_mix_key, "seq", scatter_dimension=0, tiled=True),
        lax.psum_scatter(grad_mix_value, "seq", scatter_dimension=0, tiled=True),
        lax.psum_scatter(grad_mix_recep, "seq", scatter_dimension=0, tiled=True),
        lax.psum_scatter(grad_time_decay, "seq", scatter_dimension=0, tiled=True),
        lax.psum_scatter(reward_slope_array, "seq", scatter_dimension=0, tiled=True),
        lax.psum_scatter(grad_key_weight, "seq", scatter_dimension=0, tiled=True),
        lax.psum_scatter(grad_value_weight, "seq", scatter_dimension=0, tiled=True),
        lax.psum_scatter(grad_recep_weight, "seq", scatter_dimension=0, tiled=True),
        lax.psum_scatter(grad_output_weight, "seq", scatter_dimension=0, tiled=True),
        lax.psum_scatter(grad_ffn_ln_gain, "seq", scatter_dimension=0, tiled=True),
        lax.psum_scatter(grad_ffn_ln_bias, "seq", scatter_dimension=0, tiled=True),
        lax.psum_scatter(grad_ffn_mix_key, "seq", scatter_dimension=0, tiled=True),
        lax.psum_scatter(grad_ffn_mix_recep, "seq", scatter_dimension=0, tiled=True),
        lax.psum_scatter(grad_ffn_key_weight, "seq", scatter_dimension=0, tiled=True),
        lax.psum_scatter(grad_ffn_value_weight, "seq", scatter_dimension=0, tiled=True),
        lax.psum_scatter(grad_ffn_recep_weight, "seq", scatter_dimension=0, tiled=True),
    )
    totals = lax.psum(
        (
            shares[0],
            shares[1],
            shares[2],
            shares[3],
            shares[4],
            shares[5],
            shares[6],
            shares[7],
            shares[8],
            shares[9],
            shares[10],
            shares[11],
            shares[12],
            shares[13],
            shares[14],
            shares[15],
            shares[16],
            shares[17],
        ),
        "batch",
    )
    return (
        layer_out,
        grad_tokens,
        totals[0],
        totals[1],
        totals[2],
        totals[3],
        totals[4],
        totals[5],
        totals[6],
        totals[7],
        totals[8],
        totals[9],
        totals[10],
        totals[11],
        totals[12],
        totals[13],
        totals[14],
        totals[15],
        totals[16],
        totals[17],
    )


def solution(mesh):
    return jax.shard_map(
        shards,
        mesh=mesh,
        in_specs=(
            P("batch", "seq", None),
            P("batch", None),
            P(),
            P(),
            P(),
            P(),
            P(),
            P(),
            P(),
            P(),
            P(),
            P(),
            P(),
            P(),
            P(),
            P(),
            P(),
            P(),
            P(),
            P(),
            P("batch", "seq", None),
        ),
        out_specs=(
            P("batch", "seq", None),
            P("batch", "seq", None),
            P("seq"),
            P("seq"),
            P("seq"),
            P("seq"),
            P("seq"),
            P("seq"),
            P("seq"),
            P("seq", None),
            P("seq", None),
            P("seq", None),
            P("seq", None),
            P("seq"),
            P("seq"),
            P("seq"),
            P("seq"),
            P("seq", None),
            P("seq", None),
            P("seq", None),
        ),
        check_vma=False,
    )
```

profile of v0, /device:TPU:0, one launch (start us, length us, event | category | flops | bytes accessed | tf_op | source)
XLA Modules:
  0.0 1577.8 jit_solution(16790272097540365786)
XLA Ops:
  13.0 5.5 collective-permute-start
  35.2 32.5 %all_gather.32 = f32[8,2,1024]{2,1,0:T(2,128)} all-gather(f32[1,2,1024]{2,1,0:T(2,128)S(1)} %get-tuple-element.683), channel_id=1, replica_groups=mesh['seq'=8,'batch'=4] {'seq'}, dimensions={0}, use_global_device_ids=true | all-gather | bytes 73728 | tf_op jit(solution)/shard_map/all_gather | solution.py:15
  82.0 35.9 %while.66 = (s32[]{:T(128)}, f32[2,1024]{1,0:T(2,128)S(1)}, f32[2,1024]{1,0:T(2,128)S(1)}, f32[16,2,1024]{2,1,0:T(2,128)}, f32[16,2,1024]{2,1,0:T(2,128)}, /*ind...) while((s32[]{:T(128)}, f32[2,1024]{1,0:T(2,128)S(1)}, ...), condition=%wide.region_8.9_spmd.clone, body=%wide.region_7.8_spmd.clone.sunk | while | flops 16387 | bytes 123012 | solution.py:108
  119.5 32.5 %all-gather.4 = f32[8,2,1024]{2,1,0:T(2,128)} all-gather(f32[1,2,1024]{2,1,0:T(2,128)S(1)} %bitcast.294), channel_id=2, replica_groups=mesh['seq'=8,'batch'=4] {'seq'}, dimensions={0}, use_global_device_ids=true | all-gather | bytes 73728 | tf_op jit(solution)/shard_map/all_gather | solution.py:15
  152.0 32.7 %all-gather.5 = f32[8,2,1024]{2,1,0:T(2,128)} all-gather(f32[1,2,1024]{2,1,0:T(2,128)S(1)} %bitcast.293), channel_id=3, replica_groups=mesh['seq'=8,'batch'=4] {'seq'}, dimensions={0}, use_global_device_ids=true | all-gather | bytes 73728 | tf_op jit(solution)/shard_map/all_gather | solution.py:15
  184.7 9.6 while.67
  197.8 26.6 %multiply_reduce_fusion.2 = (f32[2,16,1024,16]{2,3,1,0:T(8,128)S(1)}, f32[2,16,1024,16]{2,3,1,0:T(8,128)S(1)}) fusion(f32[2,16,1024,16]{2,3,1,0:T(8,128)S(1)} %bitcast.292, f32[16,16,1024]{2,1,0:T(8,128)S(1)} %copy-done.13, f32[2,16,16,16]{3,2,1,0:T(8,128)S(1)} %copy-done.55, f32[2,16,1024,16]{2,3,1,0:T(8,128)S(1)} %bitcast.291), kind=kLoop, calls=%fused_computation.38 | loop fusion | flops 40894464 | bytes 9469952 | tf_op jit(solution)/shard_map/rbtsd,rbsd->rbtd/dot_general | solution.py:92
  248.7 12.3 fusion.46
  271.3 13.7 multiply_convert_fusion
  285.0 8.5 fusion.12
  300.5 35.0 %all_gather.37 = f32[8,2,1024]{2,1,0:T(2,128)} all-gather(f32[1,2,1024]{2,1,0:T(2,128)S(1)} %copy-done.112), channel_id=1, replica_groups=mesh['seq'=8,'batch'=4] {'seq'}, dimensions={0}, use_global_device_ids=true | all-gather | bytes 73728 | tf_op jit(solution)/shard_map/all_gather | solution.py:15
  354.2 13.7 rev.26
  367.9 16.7 %rev.24 = f32[2,256,1024]{2,1,0:T(8,128)} reverse(f32[2,256,1024]{2,1,0:T(8,128)} %get-tuple-element.637), dimensions={1} | reverse | bytes 4194304 | tf_op jit(solution)/shard_map/rev | solution.py:253
  384.6 5.2 convolution_bitcast_fusion.3
  395.0 35.9 %while.68 = (s32[]{:T(128)}, f32[2,1024]{1,0:T(2,128)S(1)}, f32[2,1024]{1,0:T(2,128)S(1)}, f32[16,2,1024]{2,1,0:T(2,128)}, f32[16,2,1024]{2,1,0:T(2,128)}, /*ind...) while((s32[]{:T(128)}, f32[2,1024]{1,0:T(2,128)S(1)}, ...), condition=%wide.region_22.23_spmd.clone, body=%wide.region_21.22_spmd.clone.sunk | while | flops 16387 | bytes 123012 | solution.py:108
  433.8 30.7 %all-gather.7 = f32[8,2,1024]{2,1,0:T(2,128)S(1)} all-gather(f32[1,2,1024]{2,1,0:T(2,128)S(1)} %get-tuple-element.698), channel_id=5, replica_groups=mesh['seq'=8,'batch'=4] {'seq'}, dimensions={0}, use_global_device_ids=true | all-gather | bytes 73728 | tf_op jit(solution)/shard_map/all_gather | solution.py:15
  465.2 31.5 %all-gather.6 = f32[8,2,1024]{2,1,0:T(2,128)S(1)} all-gather(f32[1,2,1024]{2,1,0:T(2,128)} %get-tuple-element.699), channel_id=4, replica_groups=mesh['seq'=8,'batch'=4] {'seq'}, dimensions={0}, use_global_device_ids=true | all-gather | bytes 73728 | tf_op jit(solution)/shard_map/all_gather | solution.py:15
  498.3 27.7 %multiply_reduce_fusion = (f32[2,16,1024,16]{2,3,1,0:T(8,128)S(1)}, f32[2,16,1024,16]{2,3,1,0:T(8,128)S(1)}) fusion(f32[2,16,1024,16]{2,3,1,0:T(8,128)S(1)} %bitcast.289, f32[2,16,16,16]{3,2,1,0:T(8,128)S(1)} %get-tuple-element.693, f32[16,16,1024]{2,1,0:T(8,128)} %multiply_exponential_fusion.1, f32[2,16,1024,16]{2,3,1,0:T(8,128)} %bitcast.290), kind=kLoop, calls=%fused_computation.36 | loop fusion | flops 40894464 | bytes 9469952 | tf_op jit(solution)/shard_map/rbtsd,rbsd->rbtd/dot_general | solution.py:92
  528.6 5.4 while.69
  538.7 16.7 %rev.30 = f32[2,256,1024]{2,1,0:T(8,128)} reverse(f32[2,256,1024]{2,1,0:T(8,128)} %get-tuple-element.672), dimensions={1} | reverse | bytes 4194304 | tf_op jit(solution)/shard_map/rev | solution.py:264
  555.4 16.9 %rev.31 = f32[2,256,1024]{2,1,0:T(8,128)} reverse(f32[2,256,1024]{2,1,0:T(8,128)} %get-tuple-element.673), dimensions={1} | reverse | bytes 4194304 | tf_op jit(solution)/shard_map/rev | solution.py:265
  572.3 7.7 add_reduce_fusion
  595.2 14.4 convolution_bitcast_fusion
  610.9 10.6 convolution_bitcast_fusion.1
  621.6 52.1 %reduce-scatter.10.cloned.1.call-done = f32[128,1024]{1,0:T(8,128)} async-done(((f32[1024,1024]{1,0:T(8,128)}), f32[128,1024]{1,0:T(8,128)}) %reduce-scatter.10.cloned.1.call-update) | async-done | bytes 524304 | tf_op jit(solution)/shard_map/reduce_scatter | solution.py:321
  673.7 91.6 %reduce-scatter.8.cloned.1.call-done = f32[128,1024]{1,0:T(8,128)} async-done(((f32[1024,1024]{1,0:T(8,128)}), f32[128,1024]{1,0:T(8,128)}) %reduce-scatter.8.cloned.1.call-update) | async-done | bytes 524304 | tf_op jit(solution)/shard_map/reduce_scatter | solution.py:320
  765.3 91.3 %reduce-scatter.12.cloned.1.call-done = f32[128,1024]{1,0:T(8,128)} async-done(((f32[1024,1024]{1,0:T(8,128)}), f32[128,1024]{1,0:T(8,128)}) %reduce-scatter.12.cloned.1.call-update) | async-done | bytes 524304 | tf_op jit(solution)/shard_map/reduce_scatter | solution.py:322
  856.6 286.5 %reduce-scatter.18.cloned.1.call-done = f32[512,1024]{1,0:T(8,128)} async-done(((f32[4096,1024]{1,0:T(8,128)}), f32[512,1024]{1,0:T(8,128)}) %reduce-scatter.18.cloned.1.call-update) | async-done | bytes 2097168 | tf_op jit(solution)/shard_map/reduce_scatter | solution.py:329
  1143.2 285.5 %reduce-scatter.16.cloned.1.call-done = f32[128,4096]{1,0:T(8,128)} async-done(((f32[1024,4096]{1,0:T(8,128)}), f32[128,4096]{1,0:T(8,128)}) %reduce-scatter.16.cloned.1.call-update) | async-done | bytes 2097168 | tf_op jit(solution)/shard_map/reduce_scatter | solution.py:328
  1446.2 35.7 %all-reduce.12 = (f32[1024]{0:T(1024)S(1)}, f32[1024]{0:T(1024)S(1)}, f32[1024]{0:T(1024)S(1)}, f32[1024]{0:T(1024)S(1)}, f32[1024]{0:T(1024)S(1)}, /*index=5*/f...) all-reduce(f32[1024]{0:T(1024)S(1)} %get-tuple-element.529, ...), channel_id=6, replica_groups=mesh['seq'=8,'batch'=4] {'seq'}, use_global_device_ids=true, to_apply=%region_31.32.clone | all-reduce | flops 11264 | bytes 90112
  1482.8 7.3 all-reduce.13
  1494.1 66.3 %all-reduce.17.cloned.1.call-done = (f32[128,1024]{1,0:T(8,128)}, f32[128,1024]{1,0:T(8,128)}, f32[128,1024]{1,0:T(8,128)}, f32[128,1024]{1,0:T(8,128)}, f32[128...) async-done(((f32[128,1024]{1,0:T(8,128)}, f32[128,1024]{1,0:T(8,128)}, f32[128,1024]{1,0:T(8,128)}, f32[128,1024]{1,0:T(8,128)}, f32[128,4096]{1,0:T(8,128)}, ...) | async-done | bytes 6815760 | tf_op jit(solution)/shard_map/psum | solution.py:332
  (566 shorter events, 252.8 us)
Async XLA Ops:
  7.2 226.3 %copy-start = (bf16[1024,1024]{1,0:T(8,128)(2,1)S(1)}, bf16[1024,1024]{1,0:T(8,128)(2,1)}, u32[]{:S(2)}) copy-start(bf16[1024,1024]{1,0:T(8,128)(2,1)} %param.41) | copy-start | bytes 6291460
  7.2 614.3 %reduce-scatter.20.cloned.1.call-start = ((), (), s32[]{:S(2)}) async-start(), calls=%async_computation.13 | async-start | bytes 4718592 | tf_op jit(solution)/shard_map/reduce_scatter | solution.py:330
  8.9 10.1 copy-start.128
  8.9 13.4 copy-start.100
  8.9 14.0 copy-start.121
  12.4 19.8 %copy-start.106 = (f32[1024]{0:T(1024)S(1)}, f32[1024]{0:T(1024)}, u32[]{:S(2)}) copy-start(f32[1024]{0:T(1024)} %param.34) | copy-start | bytes 12292
  12.4 19.8 %copy-start.108 = (f32[1024]{0:T(1024)S(1)}, f32[1024]{0:T(1024)}, u32[]{:S(2)}) copy-start(f32[1024]{0:T(1024)} %param.33) | copy-start | bytes 12292
  13.0 55.9 %collective-permute-start = (f32[2,1024]{1,0:T(2,128)}, f32[2,1024]{1,0:T(2,128)}, u32[]{:S(2)}, u32[]{:S(2)}) collective-permute-start(f32[2,1024]{1,0:T(2,128)} %bitcast.256), channel_id=1, source_target_pairs={{0,4},{4,8},{8,12},{12,16},{16,20},{20,24},{24,28},{1,5},{5,9},{9,... | collective-permute-start | bytes 24584 | tf_op jit(solution)/shard_map/ppermute | solution.py:10
  19.4 8.7 copy-start.72
  23.5 9.3 copy-start.88
  197.8 26.6 %copy-start.56 = (f32[2,16,1024]{2,1,0:T(8,128)S(1)}, f32[2,16,1024]{2,1,0:T(8,128)}, u32[]{:S(2)}) copy-start(f32[2,16,1024]{2,1,0:T(8,128)} %copy.137) | copy-start | bytes 393220
  197.8 26.6 %copy-start.71 = (f32[2,16,16]{2,1,0:T(8,128)S(1)}, f32[2,16,16]{2,1,0:T(8,128)}, u32[]{:S(2)}) copy-start(f32[2,16,16]{2,1,0:T(8,128)} %copy-done.70) | copy-start | bytes 6148
  234.9 13.8 copy-start.2
  236.1 2.6 collective-permute-start.1
  248.7 12.3 copy-start.12
  265.4 356.2 %reduce-scatter.14.cloned.1.call-start = ((), (), s32[]{:S(2)}) async-start(), calls=%async_computation.10 | async-start | bytes 4718592 | tf_op jit(solution)/shard_map/reduce_scatter | solution.py:323
  299.2 41.0 %collective-permute-start.2 = (f32[2,1024]{1,0:T(2,128)}, f32[2,1024]{1,0:T(2,128)}, u32[]{:S(2)}, u32[]{:S(2)}) collective-permute-start(f32[2,1024]{1,0:T(2,128)} %bitcast.258), channel_id=1, source_target_pairs={{4,0},{8,4},{12,8},{16,12},{20,16},{24,20},{28,24},{5,1},{9,5},{13... | collective-permute-start | bytes 24584 | tf_op jit(solution)/shard_map/ppermute | solution.py:10
  389.9 283.8 %reduce-scatter.10.cloned.1.call-start = ((), (), s32[]{:S(2)}) async-start(), calls=%async_computation.8 | async-start | bytes 4718592 | tf_op jit(solution)/shard_map/reduce_scatter | solution.py:321
  498.2 27.7 %copy-start.57 = (f32[2,16,1024]{2,1,0:T(8,128)S(1)}, f32[2,16,1024]{2,1,0:T(8,128)}, u32[]{:S(2)}) copy-start(f32[2,16,1024]{2,1,0:T(8,128)} %copy.144) | copy-start | bytes 393220
  498.3 27.7 %copy-start.69 = (f32[2,16,16]{2,1,0:T(8,128)S(1)}, f32[2,16,16]{2,1,0:T(8,128)}, u32[]{:S(2)}) copy-start(f32[2,16,16]{2,1,0:T(8,128)} %copy-done.68) | copy-start | bytes 6148
  555.4 16.9 %copy-start.11 = (f32[2,256,1024]{2,1,0:T(8,128)S(1)}, f32[2,256,1024]{2,1,0:T(8,128)}, u32[]{:S(2)}) copy-start(f32[2,256,1024]{2,1,0:T(8,128)} %get-tuple-element.700) | copy-start | bytes 6291460
  555.4 16.9 %copy-start.63 = (f32[2,1024]{1,0:T(2,128)S(1)}, f32[2,1024]{1,0:T(2,128)}, u32[]{:S(2)}) copy-start(f32[2,1024]{1,0:T(2,128)} %get-tuple-element.365) | copy-start | bytes 24580
  555.4 16.9 %copy-start.65 = (f32[2,1024]{1,0:T(2,128)S(1)}, f32[2,1024]{1,0:T(2,128)}, u32[]{:S(2)}) copy-start(f32[2,1024]{1,0:T(2,128)} %get-tuple-element.363) | copy-start | bytes 24580
  555.4 16.9 %copy-start.126 = (f32[1,2,2,128]{3,1,2,0:T(2,128)S(1)}, f32[1,2,2,128]{3,1,2,0:T(2,128)}, u32[]{:S(2)}) copy-start(f32[1,2,2,128]{3,1,2,0:T(2,128)} %copy.225) | copy-start | bytes 6148
  555.4 16.9 %copy-start.132 = (f32[1024]{0:T(1024)S(1)}, f32[1024]{0:T(1024)}, u32[]{:S(2)}) copy-start(f32[1024]{0:T(1024)} %param.37) | copy-start | bytes 12292
  572.3 8.7 copy-start.47
  584.3 181.0 %reduce-scatter.8.cloned.1.call-start = ((), (), s32[]{:S(2)}) async-start(), calls=%async_computation.7 | async-start | bytes 4718592 | tf_op jit(solution)/shard_map/reduce_scatter | solution.py:320
  589.2 267.4 %reduce-scatter.12.cloned.1.call-start = ((), (), s32[]{:S(2)}) async-start(), calls=%async_computation.9 | async-start | bytes 4718592 | tf_op jit(solution)/shard_map/reduce_scatter | solution.py:322
  594.0 549.1 %reduce-scatter.18.cloned.1.call-start = ((), (), s32[]{:S(2)}) async-start(), calls=%async_computation.12 | async-start | bytes 18874368 | tf_op jit(solution)/shard_map/reduce_scatter | solution.py:329
  609.7 819.0 %reduce-scatter.16.cloned.1.call-start = ((), (), s32[]{:S(2)}) async-start(), calls=%async_computation.11 | async-start | bytes 18874368 | tf_op jit(solution)/shard_map/reduce_scatter | solution.py:328
  621.5 938.9 %all-reduce.17.cloned.1.call-start = ((), (), s32[]{:S(2)}) async-start(), calls=%async_computation.14 | async-start | bytes 13631488 | tf_op jit(solution)/shard_map/psum | solution.py:332
  1436.7 5.5 collective-permute-start.3
  (124 other events, 435.9 us)
Sparse Core Ops, SparseCore 0:
  265.5 90.0 reduce-scatter.19
  390.0 90.5 reduce-scatter.13
  584.5 89.1 reduce-scatter.9
  677.6 87.6 reduce-scatter.7
  768.8 87.7 reduce-scatter.11
  860.8 282.3 reduce-scatter.17
  1147.0 281.7 reduce-scatter.15
  1431.8 128.5 all-reduce.16
where the time goes:
time: 1590 us; the launch traced here: 1580 us
  waiting for transfers between devices  878 us (55%)
  blocking collectives  238 us (15%)
  other arithmetic  170 us (11%)
  local copies, waits for them, and re-layouts  153 us (10%)
  matrix products  110 us (7%)
  between operations  17 us (1%)
    reduce_scatter x1, waiting for transfers between devices, shards(): lax.psum_scatter(grad_ffn_value_weight, 'seq', scatter_dimension=0, tiled...  287 us
    reduce_scatter x1, waiting for transfers between devices, shards(): lax.psum_scatter(grad_ffn_key_weight, 'seq', scatter_dimension=0, tiled=T...  286 us
    all_gather x6, blocking collectives, entering_2(): pieces = jax.tree.map(lambda part: lax.all_gather(part, axis), value)  195 us
    reduce_scatter x1, waiting for transfers between devices, shards(): lax.psum_scatter(grad_key_weight, 'seq', scatter_dimension=0, tiled=True)  91.6 us
    reduce_scatter x1, waiting for transfers between devices, shards(): lax.psum_scatter(grad_recep_weight, 'seq', scatter_dimension=0, tiled=True)  91.3 us
    psum x1, waiting for transfers between devices, shards(): lax.psum((shares[0], shares[1], shares[2], shares[3], shares[4], shares[5...  66.3 us
    dot_general x2, other arithmetic, block_prefix(): jnp.einsum('rbtsd,rbsd->rbtd', weights, member, precision=lax.Precision.H...  54.2 us
    reduce_scatter x1, waiting for transfers between devices, shards(): lax.psum_scatter(grad_value_weight, 'seq', scatter_dimension=0, tiled=True)  52.1 us
  transfers between devices with their start and end apart: 12, of which 8 were waited for; matrix products, arithmetic and copies ran while one was open for 18% of the time, Pallas kernels for 0%

commit v1 on v0

v1 whole, which is shorter than its diff:
```python
import functools
import math

import jax
import jax.numpy as jnp
from jax import lax
from jax.experimental import pallas as pl
from jax.experimental.pallas import tpu as pltpu
from jax.sharding import PartitionSpec as P

F32, BF16 = jnp.float32, jnp.bfloat16
STEPS = 8


def shifted(value, axis, distance):
    devices = range(lax.axis_size(axis))
    route = [(i - distance, i) for i in devices if i - distance in devices]
    return lax.ppermute(value, axis, route)


def bit_value(bit):
    axis, place = bit
    return (lax.axis_index(axis) >> place) & 1


def exchange(value, bit):
    axis, place = bit
    return lax.ppermute(value, axis, [(i, i ^ (1 << place)) for i in range(lax.axis_size(axis))])


def pick(value, index, dim):
    return lax.dynamic_index_in_dim(value, index, dim, keepdims=False)


def total_of(terms):
    return functools.reduce(lambda a, b: a + b, terms)


def axis_bits(axis):
    return [(axis, k) for k in range(int(math.log2(lax.axis_size(axis))))]


class Partial:
    def __init__(self, terms):
        self.dims = axis_bits("seq")[::-1] + axis_bits("batch")[1:]
        lead = (2,) * len(self.dims)
        self.terms = [t.reshape(*lead, -1, t.shape[-1]) for t in terms]

    def halve(self, bit):
        dim, mine = self.dims.index(bit), bit_value(bit)
        send = total_of([pick(t, 1 - mine, dim) for t in self.terms])
        got = exchange(send, bit)
        self.terms = [pick(t, mine, dim) for t in self.terms] + [got]
        self.dims.pop(dim)

    def gather(self):
        value = total_of(self.terms)
        for bit in axis_bits("batch")[:0:-1]:
            other = exchange(value, bit)
            first = bit_value(bit) == 0
            value = jnp.concatenate(
                [jnp.where(first, value, other), jnp.where(first, other, value)], axis=0
            )
        bit = ("batch", 0)
        other = exchange(value, bit)
        first = bit_value(bit) == 0
        return jnp.concatenate(
            [jnp.where(first, value, other), jnp.where(first, other, value)], axis=1
        )


def weight_grad(left_t, right):
    bit = ("batch", 0)
    half = right.shape[1] // 2
    mine = bit_value(bit)
    dot = lambda cols: lax.dot_general(
        left_t, cols, (((0,), (0,)), ((), ())), preferred_element_type=F32
    )
    theirs = dot(lax.dynamic_slice_in_dim(right, (1 - mine) * half, half, 1))
    got = exchange(theirs, bit)
    own = dot(lax.dynamic_slice_in_dim(right, mine * half, half, 1))
    return Partial([own, got])


def reduce_vectors(vectors):
    count, seq = vectors.shape[0], lax.axis_size("seq")
    bits = axis_bits("seq")
    value = jnp.swapaxes(vectors.reshape(count, seq, -1), 0, 1)
    value = value.reshape(*((2,) * len(bits)), count, -1)
    for bit in axis_bits("batch"):
        value = value + exchange(value, bit)
    for bit in bits[::-1]:
        mine = bit_value(bit)
        value = pick(value, mine, 0) + exchange(pick(value, 1 - mine, 0), bit)
    return value


def entering(tails, begins, decay_rate, group_len, backward):
    count, mine = lax.axis_size("seq"), lax.axis_index("seq")
    sign = -1 if backward else 1

    def gain(lo, hi):
        a, b = (mine + lo, mine + hi) if backward else (mine - hi + 1, mine - lo + 1)
        hit = jnp.any((begins >= a * group_len) & (begins < b * group_len), axis=1, keepdims=True)
        return jnp.where(hit, 0.0, 1.0) * jnp.exp(-float((hi - lo) * group_len) * decay_rate)[None, :]

    reach, window, before = 1, tails, None
    while reach < count:
        got = [
            (j, shifted(window, "seq", sign * j * reach)) for j in range(1, 4) if j * reach < count
        ]
        if before is None:
            before = total_of([v if j == 1 else gain(1, j) * v for j, v in got])
            seen = 1 + len(got)
            window = tails + gain(0, 1) * before if seen < count else None
        else:
            before_more = total_of([gain(1, j * reach) * v for j, v in got])
            seen = reach * (1 + len(got))
            if seen < count:
                window = window + total_of([gain(0, j * reach) * v for j, v in got])
            before = before + before_more
        reach *= 4
    return before


def scan_params():
    return pltpu.CompilerParams(vmem_limit_bytes=48 * 1024 * 1024)


def at_step(ref, row, step, length, lanes):
    return ref[row, pl.ds(step, STEPS, stride=length // STEPS), lanes]


def lane_tiles(width):
    return [slice(i, i + 128) for i in range(0, width, 128)]


def join_pieces(tails, gains, order):
    total = None
    for c in order:
        part = tails[c : c + 1]
        total = part if total is None else gains[c : c + 1] * total + part
    return total


def forward_tails_kernel(k_ref, v_ref, keep_ref, rate_ref, piece_ref, tail_ref):
    rows, length, width = k_ref.shape
    steps = length // STEPS
    tiles = lane_tiles(width)
    chains = [(r, t) for r in range(rows) for t in tiles]
    decay = [jnp.exp(-rate_ref[0:1, t]) for t in tiles]

    def step(j, carry):
        out = []
        flags = [keep_ref[r, pl.ds(j, STEPS, stride=steps), :] for r in range(rows)]
        for i, (r, t) in enumerate(chains):
            num, den, alive = carry[i]
            e = jnp.exp(at_step(k_ref, r, j, length, t))
            v = at_step(v_ref, r, j, length, t)
            f = flags[r] * decay[i % len(tiles)]
            out.append((f * num + e * v, f * den + e, alive * flags[r]))
        return tuple(out)

    zero = jnp.zeros((STEPS, 128), F32)
    done = lax.fori_loop(
        0, steps, step, tuple((zero, zero, jnp.ones((STEPS, 128), F32)) for _ in chains), unroll=4
    )
    for (r, t), (num, den, alive) in zip(chains, done):
        gains = alive * jnp.exp(-float(steps) * rate_ref[0:1, t])
        piece_ref[0, r, :, t] = num
        piece_ref[1, r, :, t] = den
        piece_ref[2, r, :, t] = gains
        tail_ref[0, r : r + 1, t] = join_pieces(num, gains, range(STEPS))
        tail_ref[1, r : r + 1, t] = join_pieces(den, gains, range(STEPS))


def forward_states_kernel(
    k_ref, v_ref, recep_ref, keep_ref, rate_ref, bonus_ref, piece_ref, enter_ref,
    num_ref, den_ref, gated_ref,
):
    rows, length, width = k_ref.shape
    steps = length // STEPS
    tiles = lane_tiles(width)
    chains = [(r, t) for r in range(rows) for t in tiles]
    decay = [jnp.exp(-rate_ref[0:1, t]) for t in tiles]
    carry = []
    for r, t in chains:
        gains = piece_ref[2, r, :, t]
        start = []
        for q in range(2):
            tails, held, parts = piece_ref[q, r, :, t], enter_ref[q, r : r + 1, t], []
            for c in range(STEPS):
                parts.append(held)
                held = gains[c : c + 1] * held + tails[c : c + 1]
            start.append(jnp.concatenate(parts, axis=0))
        carry.append(tuple(start))

    def step(j, carry):
        out = []
        flags = [keep_ref[r, pl.ds(j, STEPS, stride=steps), :] for r in range(rows)]
        for i, (r, t) in enumerate(chains):
            num, den = carry[i]
            num, den = num * flags[r], den * flags[r]
            num_ref[r, pl.ds(j, STEPS, stride=steps), t] = num
            den_ref[r, pl.ds(j, STEPS, stride=steps), t] = den
            e = jnp.exp(at_step(k_ref, r, j, length, t))
            v = at_step(v_ref, r, j, length, t)
            d = decay[i % len(tiles)]
            out.append((d * num + e * v, d * den + e))
        return tuple(out)

    lax.fori_loop(0, steps, step, tuple(carry), unroll=4)
    bonus = bonus_ref[0:1, :]

    def finish(b, _):
        for r in range(rows):
            at = pl.ds(pl.multiple_of(b * 16, 16), 16)
            first = jnp.exp(bonus + k_ref[r, at, :])
            wkv = (num_ref[r, at, :] + first * v_ref[r, at, :]) / (den_ref[r, at, :] + first)
            gated_ref[r, at, :] = (jax.nn.sigmoid(recep_ref[r, at, :]) * wkv).astype(BF16)
        return 0

    lax.fori_loop(0, length // 16, finish, 0)


def backward_tails_kernel(
    grad_ref, k_ref, v_ref, recep_ref, num_ref, den_ref, keep_ref, rate_ref, bonus_ref,
    gnum_ref, gden_ref, grecep_ref, piece_ref, tail_ref,
):
    rows, length, width = k_ref.shape
    steps = length // STEPS
    tiles = lane_tiles(width)
    bonus = bonus_ref[0:1, :]

    def begin(b, _):
        for r in range(rows):
            at = pl.ds(pl.multiple_of(b * 16, 16), 16)
            first = jnp.exp(bonus + k_ref[r, at, :])
            below = den_ref[r, at, :] + first
            wkv = (num_ref[r, at, :] + first * v_ref[r, at, :]) / below
            gate = jax.nn.sigmoid(recep_ref[r, at, :])
            grad = grad_ref[r, at, :]
            grecep_ref[r, at, :] = (grad * wkv * (gate * (1.0 - gate))).astype(BF16)
            up = grad * gate / below
            gnum_ref[r, at, :] = up
            gden_ref[r, at, :] = -up * wkv
        return 0

    lax.fori_loop(0, length // 16, begin, 0)
    chains = [(r, t) for r in range(rows) for t in tiles]
    decay = [jnp.exp(-rate_ref[0:1, t]) for t in tiles]

    def step(i_step, carry):
        j = steps - 1 - i_step
        out = []
        flags = [keep_ref[r, pl.ds(j, STEPS, stride=steps), :] for r in range(rows)]
        for i, (r, t) in enumerate(chains):
            num, den, alive = carry[i]
            d = decay[i % len(tiles)]
            out.append(
                (
                    flags[r] * (at_step(gnum_ref, r, j, length, t) + d * num),
                    flags[r] * (at_step(gden_ref, r, j, length, t) + d * den),
                    alive * flags[r],
                )
            )
        return tuple(out)

    zero = jnp.zeros((STEPS, 128), F32)
    done = lax.fori_loop(
        0, steps, step, tuple((zero, zero, jnp.ones((STEPS, 128), F32)) for _ in chains), unroll=4
    )
    for (r, t), (num, den, alive) in zip(chains, done):
        gains = alive * jnp.exp(-float(steps) * rate_ref[0:1, t])
        piece_ref[0, r, :, t] = num
        piece_ref[1, r, :, t] = den
        piece_ref[2, r, :, t] = gains
        tail_ref[0, r : r + 1, t] = join_pieces(num, gains, range(STEPS)[::-1])
        tail_ref[1, r : r + 1, t] = join_pieces(den, gains, range(STEPS)[::-1])


def backward_states_kernel(
    gnum_ref, gden_ref, k_ref, v_ref, num_ref, den_ref, keep_ref, rate_ref, bonus_ref, piece_ref,
    enter_ref, gkey_ref, gvalue_ref, sums_ref, snum_ref, sden_ref,
):
    rows, length, width = k_ref.shape
    steps = length // STEPS
    tiles = lane_tiles(width)
    chains = [(r, t) for r in range(rows) for t in tiles]
    decay = [jnp.exp(-rate_ref[0:1, t]) for t in tiles]
    carry = []
    for r, t in chains:
        gains = piece_ref[2, r, :, t]
        start = []
        for q in range(2):
            tails, held, parts = piece_ref[q, r, :, t], enter_ref[q, r : r + 1, t], []
            for c in range(STEPS)[::-1]:
                parts.append(held)
                held = gains[c : c + 1] * held + tails[c : c + 1]
            start.append(jnp.concatenate(parts[::-1], axis=0))
        carry.append(tuple(start))

    def step(i_step, carry):
        j = steps - 1 - i_step
        out = []
        flags = [keep_ref[r, pl.ds(j, STEPS, stride=steps), :] for r in range(rows)]
        for i, (r, t) in enumerate(chains):
            num, den = carry[i]
            snum_ref[r, pl.ds(j, STEPS, stride=steps), t] = num
            sden_ref[r, pl.ds(j, STEPS, stride=steps), t] = den
            d = decay[i % len(tiles)]
            out.append(
                (
                    flags[r] * (at_step(gnum_ref, r, j, length, t) + d * num),
                    flags[r] * (at_step(gden_ref, r, j, length, t) + d * den),
                )
            )
        return tuple(out)

    lax.fori_loop(0, steps, step, tuple(carry), unroll=4)
    bonus = bonus_ref[0:1, :]

    def finish(b, sums):
        slope, fade = sums
        for r in range(rows):
            at = pl.ds(pl.multiple_of(b * 16, 16), 16)
            key, value = k_ref[r, at, :], v_ref[r, at, :]
            e, first = jnp.exp(key), jnp.exp(bonus + key)
            up, low = gnum_ref[r, at, :], gden_ref[r, at, :]
            later_num, later_den = snum_ref[r, at, :], sden_ref[r, at, :]
            present = first * (up * value + low)
            gvalue_ref[r, at, :] = (up * first + later_num * e).astype(BF16)
            gkey_ref[r, at, :] = (present + e * (later_num * value + later_den)).astype(BF16)
            slope = slope + present[:8] + present[8:]
            both = num_ref[r, at, :] * later_num + den_ref[r, at, :] * later_den
            fade = fade + both[:8] + both[8:]
        return slope, fade

    zero = jnp.zeros((8, width), F32)
    slope, fade = lax.fori_loop(0, length // 16, finish, (zero, zero))
    sums_ref[0:8, :] = slope
    sums_ref[8:16, :] = fade


def scan_call(kernel, inputs, outputs, scratch=(), width=128):
    features = inputs[0].shape[-1]

    def spec(shape):
        lead = len(shape) - 1
        if shape[-1] == 128 and features != 128:
            return pl.BlockSpec(shape, lambda i: (0,) * (lead + 1))
        return pl.BlockSpec((*shape[:-1], width), lambda i: (0,) * lead + (i,))

    out_shape = [jax.ShapeDtypeStruct(s, d) for s, d in outputs]
    moved = sum(x.size * x.dtype.itemsize for x in [*inputs, *out_shape])
    return pl.pallas_call(
        kernel,
        out_shape=out_shape,
        grid=(features // width,),
        in_specs=[spec(x.shape) for x in inputs],
        out_specs=[spec(s) for s, _ in outputs],
        scratch_shapes=[pltpu.VMEM((*s[:-1], width), F32) for s in scratch],
        compiler_params=scan_params(),
        cost_estimate=pl.CostEstimate(
            flops=20 * inputs[0].size, bytes_accessed=moved, transcendentals=inputs[0].size
        ),
    )(*inputs)


def norm_rows(value_rows, gain_vec, bias_vec):
    row_mean = jnp.mean(value_rows, axis=-1, keepdims=True)
    centred = value_rows - row_mean
    inv_std = lax.rsqrt(jnp.mean(centred * centred, axis=-1, keepdims=True) + 1e-05)
    normed = centred * inv_std
    return (normed * gain_vec + bias_vec, normed, inv_std)


def norm_back(grad_in, normed, inv_std, gain_vec):
    scaled = grad_in * gain_vec
    return inv_std * (
        scaled
        - jnp.mean(scaled, axis=-1, keepdims=True)
        - normed * jnp.mean(scaled * normed, axis=-1, keepdims=True)
    )


def project(left_side, right_side):
    return jnp.einsum("rcd,de->rce", left_side, right_side, preferred_element_type=F32)


def project_back(grad_in, right_side):
    return jnp.einsum("rce,de->rcd", grad_in, right_side, preferred_element_type=F32)


def with_previous(value_rows, edge_row, keep):
    earlier = jnp.concatenate([edge_row[:, None, :], value_rows[:, :-1, :]], axis=1)
    return earlier * keep[:, :, None]


def flat(value):
    return value.reshape(-1, value.shape[-1])


def shards(
    incoming_symbols,
    article_sizes,
    mixer_norm_scale,
    mixer_norm_offset,
    temporal_lookup_share,
    temporal_payload_share,
    temporal_gate_share,
    fading_log_rates,
    present_reward_vector,
    lookup_matrix,
    payload_matrix,
    gate_matrix,
    emission_matrix,
    channel_norm_scale,
    channel_norm_offset,
    channel_lookup_share,
    channel_gate_share,
    channel_lookup_matrix,
    channel_payload_matrix,
    channel_gate_matrix,
    final_cotangent,
):
    rows_here, group_len, features = incoming_symbols.shape
    full = (rows_here, group_len, features)
    begins = jnp.cumsum(article_sizes, axis=1) - article_sizes
    position = lax.axis_index("seq") * group_len + jnp.arange(group_len, dtype=jnp.int32)
    starts = jnp.any(position[None, :, None] == begins[:, None, :], axis=2)
    keep = jnp.where(starts, 0.0, 1.0).astype(F32)
    keep_wide = jnp.broadcast_to(keep[:, :, None], (rows_here, group_len, 128))
    decay_rate = jnp.exp(fading_log_rates)
    rate_row = jnp.broadcast_to(decay_rate[None, :], (8, features))
    bonus_row = jnp.broadcast_to(present_reward_vector[None, :], (8, features))
    enter = functools.partial(entering, begins=begins, decay_rate=decay_rate, group_len=group_len)

    symbols = incoming_symbols.astype(F32)
    att_last = norm_rows(symbols[:, -1, :], mixer_norm_scale, mixer_norm_offset)[0]
    att_edge = shifted(att_last, "seq", 1)
    att_normed, att_unit, att_inv = norm_rows(symbols, mixer_norm_scale, mixer_norm_offset)
    att_prev = with_previous(att_normed, att_edge, keep)
    mix = lambda share: (att_normed * share + att_prev * (1.0 - share)).astype(BF16)
    key_mixed = mix(temporal_lookup_share)
    value_mixed = mix(temporal_payload_share)
    recep_mixed = mix(temporal_gate_share)
    key_proj = project(key_mixed, lookup_matrix)
    value_proj = project(value_mixed, payload_matrix)
    recep_proj = project(recep_mixed, gate_matrix)
    pieces = ((3, rows_here, STEPS, features), F32)
    tails = ((2, rows_here, features), F32)
    piece, tail = scan_call(
        forward_tails_kernel, [key_proj, value_proj, keep_wide, rate_row], [pieces, tails]
    )
    num_state, den_state, gated = scan_call(
        forward_states_kernel,
        [key_proj, value_proj, recep_proj, keep_wide, rate_row, bonus_row, piece, enter(tail, backward=False)],
        [(full, F32), (full, F32), (full, BF16)],
    )
    after_att = symbols + project(gated, emission_matrix)

    ffn_normed, ffn_unit, ffn_inv = norm_rows(after_att, channel_norm_scale, channel_norm_offset)
    ffn_edge = shifted(ffn_normed[:, -1, :], "seq", 1)
    ffn_prev = with_previous(ffn_normed, ffn_edge, keep)
    ffn_key_mixed = (
        ffn_normed * channel_lookup_share + ffn_prev * (1.0 - channel_lookup_share)
    ).astype(BF16)
    ffn_recep_mixed = (
        ffn_normed * channel_gate_share + ffn_prev * (1.0 - channel_gate_share)
    ).astype(BF16)
    hidden_pre = project(ffn_key_mixed, channel_lookup_matrix)
    above = jnp.maximum(hidden_pre, 0.0)
    squared = jnp.square(above).astype(BF16)
    ffn_gate = jax.nn.sigmoid(project(ffn_recep_mixed, channel_gate_matrix))
    ffn_value = project(squared, channel_payload_matrix)
    layer_out = (after_att + ffn_gate * ffn_value).astype(BF16)

    grad_top = final_cotangent.astype(F32)
    grad_fvalue = (grad_top * ffn_gate).astype(BF16)
    grad_frecep = (grad_top * ffn_value * (ffn_gate * (1.0 - ffn_gate))).astype(BF16)
    hidden = hidden_pre.shape[-1]
    value_parts = [
        weight_grad(flat(squared), flat(grad_fvalue)[:, i * features // 2 : (i + 1) * features // 2])
        for i in range(2)
    ]
    grad_squared = project_back(grad_fvalue, channel_payload_matrix)
    grad_hidden = (grad_squared * (2.0 * above)).astype(BF16)
    key_parts = [
        weight_grad(flat(ffn_key_mixed), flat(grad_hidden)[:, i * hidden // 2 : (i + 1) * hidden // 2])
        for i in range(2)
    ]
    frecep_part = weight_grad(flat(ffn_recep_mixed), flat(grad_frecep))
    grad_fkey_in = project_back(grad_hidden, channel_lookup_matrix)
    grad_frecep_in = project_back(grad_frecep, channel_gate_matrix)
    ffn_delta = ffn_normed - ffn_prev
    grad_ffn_mix_key = jnp.sum(grad_fkey_in * ffn_delta, axis=(0, 1))
    grad_ffn_mix_recep = jnp.sum(grad_frecep_in * ffn_delta, axis=(0, 1))
    grad_ffn_prev = (
        grad_fkey_in * (1.0 - channel_lookup_share) + grad_frecep_in * (1.0 - channel_gate_share)
    ) * keep[:, :, None]
    ffn_back_edge = shifted(grad_ffn_prev[:, 0, :], "seq", -1)
    grad_ffn_normed = (
        grad_fkey_in * channel_lookup_share
        + grad_frecep_in * channel_gate_share
        + jnp.concatenate([grad_ffn_prev[:, 1:, :], ffn_back_edge[:, None, :]], axis=1)
    )
    grad_ffn_ln_gain = jnp.sum(grad_ffn_normed * ffn_unit, axis=(0, 1))
    grad_ffn_ln_bias = jnp.sum(grad_ffn_normed, axis=(0, 1))
    grad_after = grad_top + norm_back(grad_ffn_normed, ffn_unit, ffn_inv, channel_norm_scale)

    grad_att_out = grad_after.astype(BF16)
    output_part = weight_grad(flat(gated), flat(grad_att_out))
    grad_gated = project_back(grad_att_out, emission_matrix)
    grad_num, grad_den, grad_recep, piece, tail = scan_call(
        backward_tails_kernel,
        [grad_gated, key_proj, value_proj, recep_proj, num_state, den_state, keep_wide, rate_row, bonus_row],
        [(full, F32), (full, F32), (full, BF16), pieces, tails],
    )
    grad_key, grad_value, sums = scan_call(
        backward_states_kernel,
        [grad_num, grad_den, key_proj, value_proj, num_state, den_state, keep_wide, rate_row, bonus_row, piece, enter(tail, backward=True)],
        [(full, BF16), (full, BF16), ((16, features), F32)],
        scratch=(full, full),
    )
    reward_slope = jnp.sum(sums[:8], axis=0)
    grad_time_decay = -decay_rate * jnp.exp(-decay_rate) * jnp.sum(sums[8:], axis=0)
    att_parts = [
        weight_grad(flat(recep_mixed), flat(grad_recep)),
        weight_grad(flat(key_mixed), flat(grad_key)),
        weight_grad(flat(value_mixed), flat(grad_value)),
    ]
    grad_key_in = project_back(grad_key, lookup_matrix)
    grad_value_in = project_back(grad_value, payload_matrix)
    grad_recep_in = project_back(grad_recep, gate_matrix)
    att_delta = att_normed - att_prev
    grad_mix_key = jnp.sum(grad_key_in * att_delta, axis=(0, 1))
    grad_mix_value = jnp.sum(grad_value_in * att_delta, axis=(0, 1))
    grad_mix_recep = jnp.sum(grad_recep_in * att_delta, axis=(0, 1))
    grad_att_prev = (
        grad_key_in * (1.0 - temporal_lookup_share)
        + grad_value_in * (1.0 - temporal_payload_share)
        + grad_recep_in * (1.0 - temporal_gate_share)
    ) * keep[:, :, None]
    att_back_edge = shifted(grad_att_prev[:, 0, :], "seq", -1)
    grad_att_normed = (
        grad_key_in * temporal_lookup_share
        + grad_value_in * temporal_payload_share
        + grad_recep_in * temporal_gate_share
        + jnp.concatenate([grad_att_prev[:, 1:, :], att_back_edge[:, None, :]], axis=1)
    )
    grad_att_ln_gain = jnp.sum(grad_att_normed * att_unit, axis=(0, 1))
    grad_att_ln_bias = jnp.sum(grad_att_normed, axis=(0, 1))
    grad_tokens = (
        grad_after + norm_back(grad_att_normed, att_unit, att_inv, mixer_norm_scale)
    ).astype(BF16)

    seq_bits, batch_bits = axis_bits("seq"), axis_bits("batch")[1:]
    plane_a = batch_bits + seq_bits
    plane_b = seq_bits[:1] + batch_bits + seq_bits[1:]
    far = seq_bits[1:] + batch_bits + seq_bits[:1]
    jobs = [
        (value_parts[0], plane_a),
        (value_parts[1], plane_b),
        (key_parts[0], plane_a),
        (key_parts[1], plane_b),
        (frecep_part, far),
        (output_part, far),
        (att_parts[0], plane_a),
        (att_parts[1], plane_b),
        (att_parts[2], plane_a),
    ]
    for part, order in jobs:
        for bit in order:
            part.halve(bit)
    done = [part.gather() for part, _ in jobs]
    vectors = jnp.stack(
        [
            grad_att_ln_gain,
            grad_att_ln_bias,
            grad_mix_key,
            grad_mix_value,
            grad_mix_recep,
            grad_time_decay,
            reward_slope,
            grad_ffn_ln_gain,
            grad_ffn_ln_bias,
            grad_ffn_mix_key,
            grad_ffn_mix_recep,
        ]
    )
    small = reduce_vectors(vectors)
    return (
        layer_out,
        grad_tokens,
        *[small[i] for i in range(7)],
        done[7],
        done[8],
        done[6],
        done[5],
        *[small[i] for i in range(7, 11)],
        jnp.concatenate(done[2:4], axis=1),
        jnp.concatenate(done[0:2], axis=1),
        done[4],
    )


def solution(mesh):
    tokens = P("batch", "seq", None)
    vector, matrix = P("seq"), P("seq", None)
    return jax.shard_map(
        shards,
        mesh=mesh,
        in_specs=(tokens, P("batch", None), *([P()] * 18), tokens),
        out_specs=(tokens, tokens, *([vector] * 7), *([matrix] * 4), *([vector] * 4), *([matrix] * 3)),
        check_vma=False,
    )
```

time: 1590 us -> 664 us (0.42)
  waiting for transfers between devices: 878 us -> 315 us
  blocking collectives: 238 us -> 0 us
  local copies, waits for them, and re-layouts: 153 us -> 38.8 us
  other arithmetic: 170 us -> 82.3 us
  starting transfers between devices: 10.9 us -> 79.8 us
  Pallas kernels: 0 us -> 43.2 us
  matrix products: 110 us -> 93.8 us
    reduce_scatter x7 -> x0, waiting for transfers between devices: 807 us -> none  [the longest x1 287 us: shards(): lax.psum_scatter(grad_ffn_value_weight, 'seq', scatter_dimension=0, tiled...]
    ppermute x4 -> x80, waiting for transfers between devices: 4.49 us -> 315 us  [the longest x68 304 us: exchange(): lax.ppermute(value, axis, [(i, i ^ 1 << place) for i in range(lax.axis_si...]
    all_gather x6 -> x0, blocking collectives: 195 us -> none  [entering_2(): pieces = jax.tree.map(lambda part: lax.all_gather(part, axis), value)]
    ppermute x4 -> x80, starting transfers between devices: 9.86 us -> 79.8 us  [the longest x68 49.3 us: exchange(): lax.ppermute(value, axis, [(i, i ^ 1 << place) for i in range(lax.axis_si...]
    rev x7 -> x0, local copies, waits for them, and re-layouts: 66.7 us -> none  [the longest x1 16.9 us: shards(): trailing_denominator = back_den[:, ::-1, :]]
    psum x1 -> x0, waiting for transfers between devices: 66.3 us -> none  [shards(): lax.psum((shares[0], shares[1], shares[2], shares[3], shares[4], shares[5...]
    dot_general x2 -> x0, other arithmetic: 54.2 us -> none  [block_prefix(): jnp.einsum('rbtsd,rbsd->rbtd', weights, member, precision=lax.Precision.H...]
    pallas_call x0 -> x4, Pallas kernels: none -> 43.2 us  [scan_call(): pl.pallas_call(kernel, out_shape=out_shape, grid=(features // width,), in...]
  transfers between devices with their start and end apart: 12 -> 80, of which waited for: 8 -> 38; matrix products, arithmetic and copies ran while one was open for 18% -> 19% of each run, Pallas kernels for 0% -> 4%
where the time goes in v1:
time: 664 us; the launch traced here: 656 us
  waiting for transfers between devices  315 us (47%)
  matrix products  93.8 us (14%)
  other arithmetic  82.3 us (12%)
  starting transfers between devices  79.8 us (12%)
  Pallas kernels  43.2 us (7%)
  local copies, waits for them, and re-layouts  38.8 us (6%)
    ppermute x68, waiting for transfers between devices, exchange(): lax.ppermute(value, axis, [(i, i ^ 1 << place) for i in range(lax.axis_si...  304 us
    ppermute x68, starting transfers between devices, exchange(): lax.ppermute(value, axis, [(i, i ^ 1 << place) for i in range(lax.axis_si...  49.3 us
    add x45, other arithmetic, total_of(): return functools.reduce(lambda a, b: a + b, terms)  45.6 us
    pallas_call x4, Pallas kernels, scan_call(): pl.pallas_call(kernel, out_shape=out_shape, grid=(features // width,), in...  43.2 us
    dot_general x18, matrix products, weight_grad(): lax.dot_general(left_t, cols, (((0,), (0,)), ((), ())), preferred_element...  41.5 us
    ppermute x12, starting transfers between devices, shifted(): return lax.ppermute(value, axis, route)  30.5 us
    dot_general x7, matrix products, project_back(): jnp.einsum('rce,de->rcd', grad_in, right_side, preferred_element_type=F32)  26.9 us
    dot_general x7, matrix products, project(): jnp.einsum('rcd,de->rce', left_side, right_side, preferred_element_type=F32)  25.4 us
  transfers between devices with their start and end apart: 80, of which 38 were waited for; matrix products, arithmetic and copies ran while one was open for 19% of the time, Pallas kernels for 4%

profile of v1, /device:TPU:0, one launch (start us, length us, event | category | flops | bytes accessed | tf_op | source)
XLA Modules:
  0.0 655.9 jit_solution(1062083223669484697)
XLA Ops:
  3.6 4.9 collective-permute-start
  20.6 5.3 shard_map.356
  45.1 12.4 %shard_map.357 = (f32[2,256,1024]{2,1,0:T(8,128)S(1)}, f32[2,256,1024]{2,1,0:T(8,128)S(1)}, bf16[2,256,1024]{2,1,0:T(8,128)(2,1)S(1)}) custom-call(f32[2,256,1024]{2,1,0:T(8,128)} %copy-done.2, f32[2,256,1024]{2,1,0:T(8,128)} %copy-done.3, f32[2,256,1024]{2,1,0:T(8,128)} %fusion.23.recep_ref, f32[2,256,128]{2,1,0:T(8,128)S(1)} %broadcast_in_dim.47.keep_ref, ...), custom_call_target="tpu_custom_call" | custom-call | flops 10485760 | bytes 12075008 | tf_op jit(solution)/shard_map/pallas_call | solution.py:356
  78.0 11.1 %multiply_convert_fusion.1 = (bf16[2,256,4096]{2,1,0:T(8,128)(2,1)S(1)}, f32[2,256,4096]{2,1,0:T(8,128)}) fusion(bf16[2,256,1024]{2,1,0:T(8,128)(2,1)S(1)} %get-tuple-element.78, bf16[1024,4096]{1,0:T(8,128)(2,1)} %param.38), kind=kOutput, calls=%fused_computation.9 | convolution fusion | flops 4301258752 | bytes 22020096 | tf_op jit(solution)/shard_map/rcd,de->rce/dot_general | solution.py:388
  89.2 4.5 fusion.2
  99.1 6.9 %copy.130 = bf16[4096,512]{1,0:T(8,128)(2,1)} copy(bf16[4096,512]{0,1:T(8,128)(2,1)} %bitcast.615) | data formatting | bytes 8388608 | tf_op jit(solution)/shard_map/dot_general | solution.py:76
  106.0 5.7 fusion.82
  121.7 9.5 %multiply_convert_fusion = bf16[2,256,4096]{2,1,0:T(8,128)(2,1)S(1)} fusion(f32[2,256,4096]{2,1,0:T(8,128)} %get-tuple-element.152, bf16[2,256,1024]{2,1,0:T(8,128)(2,1)S(1)} %copy-done.60, bf16[4096,1024]{1,0:T(8,128)(2,1)} %param.39), kind=kOutput, calls=%fused_computation.8 | convolution fusion | flops 4303355904 | bytes 22020096 | tf_op jit(solution)/shard_map/rce,de->rcd/dot_general | solution.py:392
  131.2 7.1 %fusion.4 = f32[2,256,1024]{2,1,0:T(8,128)S(1)} fusion(bf16[2,256,4096]{2,1,0:T(8,128)(2,1)S(1)} %multiply_convert_fusion, bf16[1024,4096]{1,0:T(8,128)(2,1)} %param.38), kind=kOutput, calls=%fused_computation.4 | convolution fusion | flops 4294967296 | bytes 14680064 | tf_op jit(solution)/shard_map/rce,de->rcd/dot_general | solution.py:392
  158.4 5.0 multiply_reduce_fusion.2
  168.4 12.6 %shard_map.358 = (f32[2,256,1024]{2,1,0:T(8,128)S(1)}, f32[2,256,1024]{2,1,0:T(8,128)S(1)}, bf16[2,256,1024]{2,1,0:T(8,128)(2,1)S(1)}, f32[3,2,8,1024]{3,2,1,0:T(8,128)S(1)}, f32[2,2,1024]{2,1,0:T(2,128)S(1)}) custom-call(f32[2,256,1024]{2,1,0:T(8,128)} %fusion.17.grad_ref, f32[2,256,1024]{2,1,0:T(8,128)} %copy-done.2, f32[2,256,1024]{2,1,0:T(8,128)} %copy-done.3, ...), custom_call_target="tpu_custom_call" | custom-call | flops 10485760 | bytes 18366464 | tf_op jit(solution)/shard_map/pallas_call | solution.py:356
  198.7 12.9 %shard_map.359 = (bf16[2,256,1024]{2,1,0:T(8,128)(2,1)S(1)}, bf16[2,256,1024]{2,1,0:T(8,128)(2,1)S(1)}, f32[16,1024]{1,0:T(8,128)S(1)}) custom-call(f32[2,256,1024]{2,1,0:T(8,128)S(1)} %get-tuple-element.38.gnum_ref, f32[2,256,1024]{2,1,0:T(8,128)} %copy-done.6, f32[2,256,1024]{2,1,0:T(8,128)} %copy-done.2, f32[2,256,1024]{2,1,0:T(8,128)} %copy-done.3, ...), custom_call_target="tpu_custom_call" | custom-call | flops 10485760 | bytes 15286272 | tf_op jit(solution)/shard_map/pallas_call | solution.py:356
  221.9 4.7 multiply_reduce_fusion.6
  240.6 5.3 collective-permute-start.14
  256.0 39.4 %collective-permute-done.15 = f32[2,11,128]{2,1,0:T(8,128)S(1)} collective-permute-done((f32[2,11,128]{2,1,0:T(8,128)S(1)}, f32[2,11,128]{2,1,0:T(8,128)S(1)}, u32[]{:S(2)}, u32[]{:S(2)}) %collective-permute-start.15) | collective-permute-done | bytes 11296 | tf_op jit(solution)/shard_map/ppermute | solution.py:28
  309.2 12.4 %collective-permute-done.25 = f32[2,2,2,64,512]{4,3,2,1,0:T(8,128)S(1)} collective-permute-done((f32[2,2,2,64,512]{4,3,2,1,0:T(8,128)S(1)}, f32[2,2,2,64,512]{4,3,2,1,0:T(8,128)S(1)}, u32[]{:S(2)}, u32[]{:S(2)}) %collective-permute-start.25) | collective-permute-done | bytes 1048608 | tf_op jit(solution)/shard_map/ppermute | solution.py:28
  322.7 12.5 %collective-permute-done.75 = f32[2,2,64,512]{3,2,1,0:T(8,128)S(1)} collective-permute-done((f32[2,2,64,512]{3,2,1,0:T(8,128)S(1)}, f32[2,2,64,512]{3,2,1,0:T(8,128)S(1)}, u32[]{:S(2)}, u32[]{:S(2)}) %collective-permute-start.75) | collective-permute-done | bytes 524320 | tf_op jit(solution)/shard_map/ppermute | solution.py:28
  335.8 10.5 %collective-permute-done.40 = f32[2,2,64,512]{3,2,1,0:T(8,128)S(1)} collective-permute-done((f32[2,2,64,512]{3,2,1,0:T(8,128)S(1)}, f32[2,2,64,512]{3,2,1,0:T(8,128)S(1)}, u32[]{:S(2)}, u32[]{:S(2)}) %collective-permute-start.40) | collective-permute-done | bytes 524320 | tf_op jit(solution)/shard_map/ppermute | solution.py:28
  352.1 9.1 %collective-permute-done.26 = f32[2,2,64,512]{3,2,1,0:T(8,128)} collective-permute-done((f32[2,2,64,512]{3,2,1,0:T(8,128)}, f32[2,2,64,512]{3,2,1,0:T(8,128)}, u32[]{:S(2)}, u32[]{:S(2)}) %collective-permute-start.26) | collective-permute-done | bytes 524320 | tf_op jit(solution)/shard_map/ppermute | solution.py:28
  363.5 5.0 collective-permute-done.76
  377.7 4.7 collective-permute-done.41
  384.3 7.1 %collective-permute-done.20 = f32[2,64,512]{2,1,0:T(8,128)S(1)} collective-permute-done((f32[2,64,512]{2,1,0:T(8,128)S(1)}, f32[2,64,512]{2,1,0:T(8,128)S(1)}, u32[]{:S(2)}, u32[]{:S(2)}) %collective-permute-start.20) | collective-permute-done | bytes 262176 | tf_op jit(solution)/shard_map/ppermute | solution.py:28
  403.8 8.4 %collective-permute-done.35 = f32[64,512]{1,0:T(8,128)S(1)} collective-permute-done((f32[64,512]{1,0:T(8,128)S(1)}, f32[64,512]{1,0:T(8,128)S(1)}, u32[]{:S(2)}, u32[]{:S(2)}) %collective-permute-start.35) | collective-permute-done | bytes 131104 | tf_op jit(solution)/shard_map/ppermute | solution.py:28
  418.1 4.8 collective-permute-done.21
  424.1 4.7 collective-permute-done.28
  446.4 82.4 %collective-permute-done.29 = f32[64,512]{1,0:T(8,128)S(1)} collective-permute-done((f32[64,512]{1,0:T(8,128)S(1)}, f32[64,512]{1,0:T(8,128)S(1)}, u32[]{:S(2)}, u32[]{:S(2)}) %collective-permute-start.29) | collective-permute-done | bytes 131104 | tf_op jit(solution)/shard_map/ppermute | solution.py:28
  543.8 17.4 %collective-permute-done.54 = f32[2,2,64,1024]{3,2,1,0:T(8,128)S(1)} collective-permute-done((f32[2,2,64,1024]{3,2,1,0:T(8,128)S(1)}, f32[2,2,64,1024]{3,2,1,0:T(8,128)S(1)}, u32[]{:S(2)}, u32[]{:S(2)}) %collective-permute-start.54) | collective-permute-done | bytes 1048608 | tf_op jit(solution)/shard_map/ppermute | solution.py:28
  565.7 17.4 %collective-permute-done.68 = f32[2,2,256,256]{3,2,1,0:T(8,128)S(1)} collective-permute-done((f32[2,2,256,256]{3,2,1,0:T(8,128)S(1)}, f32[2,2,256,256]{3,2,1,0:T(8,128)S(1)}, u32[]{:S(2)}, u32[]{:S(2)}) %collective-permute-start.68) | collective-permute-done | bytes 1048608 | tf_op jit(solution)/shard_map/ppermute | solution.py:28
  592.3 17.6 %collective-permute-done.69 = f32[2,256,256]{2,1,0:T(8,128)S(1)} collective-permute-done((f32[2,256,256]{2,1,0:T(8,128)S(1)}, f32[2,256,256]{2,1,0:T(8,128)S(1)}, u32[]{:S(2)}, u32[]{:S(2)}) %collective-permute-start.69) | collective-permute-done | bytes 524320 | tf_op jit(solution)/shard_map/ppermute | solution.py:28
  610.1 10.2 %collective-permute-done.62 = f32[2,256,256]{2,1,0:T(8,128)S(1)} collective-permute-done((f32[2,256,256]{2,1,0:T(8,128)S(1)}, f32[2,256,256]{2,1,0:T(8,128)S(1)}, u32[]{:S(2)}, u32[]{:S(2)}) %collective-permute-start.62) | collective-permute-done | bytes 524320 | tf_op jit(solution)/shard_map/ppermute | solution.py:28
  624.8 12.2 %collective-permute-done.70 = f32[256,256]{1,0:T(8,128)S(1)} collective-permute-done((f32[256,256]{1,0:T(8,128)S(1)}, f32[256,256]{1,0:T(8,128)S(1)}, u32[]{:S(2)}, u32[]{:S(2)}) %collective-permute-start.70) | collective-permute-done | bytes 262176 | tf_op jit(solution)/shard_map/ppermute | solution.py:28
  645.5 5.5 collective-permute-done.64
  (554 shorter events, 263.3 us)
Async XLA Ops:
  155.2 85.4 %collective-permute-start.73 = (f32[1024,512]{1,0:T(8,128)}, f32[1024,512]{1,0:T(8,128)}, u32[]{:S(2)}, u32[]{:S(2)}) collective-permute-start(f32[1024,512]{1,0:T(8,128)} %fusion.59), channel_id=1, source_target_pairs={{0,1},{1,0},{2,3},{3,2},{4,5},{5,4},{6,7},{7,6},{8,9},{9,8},{10,11... | collective-permute-start | bytes 6291464 | tf_op jit(solution)/shard_map/ppermute | solution.py:28
  187.0 60.3 %collective-permute-start.31 = (f32[1024,512]{1,0:T(8,128)}, f32[1024,512]{1,0:T(8,128)}, u32[]{:S(2)}, u32[]{:S(2)}) collective-permute-start(f32[1024,512]{1,0:T(8,128)} %fusion.65), channel_id=1, source_target_pairs={{0,1},{1,0},{2,3},{3,2},{4,5},{5,4},{6,7},{7,6},{8,9},{9,8},{10,11... | collective-permute-start | bytes 6291464 | tf_op jit(solution)/shard_map/ppermute | solution.py:28
  195.3 53.5 %collective-permute-start.38 = (f32[1024,512]{1,0:T(8,128)}, f32[1024,512]{1,0:T(8,128)}, u32[]{:S(2)}, u32[]{:S(2)}) collective-permute-start(f32[1024,512]{1,0:T(8,128)} %fusion.62), channel_id=1, source_target_pairs={{0,1},{1,0},{2,3},{3,2},{4,5},{5,4},{6,7},{7,6},{8,9},{9,8},{10,11... | collective-permute-start | bytes 6291464 | tf_op jit(solution)/shard_map/ppermute | solution.py:28
  220.0 31.8 %collective-permute-start.17 = (f32[1024,512]{1,0:T(8,128)}, f32[1024,512]{1,0:T(8,128)}, u32[]{:S(2)}, u32[]{:S(2)}) collective-permute-start(f32[1024,512]{1,0:T(8,128)} %fusion.71), channel_id=1, source_target_pairs={{0,1},{1,0},{2,3},{3,2},{4,5},{5,4},{6,7},{7,6},{8,9},{9,8},{10,11... | collective-permute-start | bytes 6291464 | tf_op jit(solution)/shard_map/ppermute | solution.py:28
  247.3 49.7 %collective-permute-start.74 = (f32[2,2,2,64,512]{4,3,2,1,0:T(8,128)S(1)}, f32[2,2,2,64,512]{4,3,2,1,0:T(8,128)S(1)}, u32[]{:S(2)}, u32[]{:S(2)}) collective-permute-start(f32[2,2,2,64,512]{4,3,2,1,0:T(8,128)S(1)} %add_bitcast_fusion.4), channel_id=1, source_target_pairs={{0,8},{4,12},{8,0},{12,4},{16,24},{20,28},{24,16},{28,20},{1,9},{5... | collective-permute-start | bytes 3145736 | tf_op jit(solution)/shard_map/ppermute | solution.py:28
  248.8 49.8 %collective-permute-start.32 = (f32[2,2,2,64,512]{4,3,2,1,0:T(8,128)S(1)}, f32[2,2,2,64,512]{4,3,2,1,0:T(8,128)S(1)}, u32[]{:S(2)}, u32[]{:S(2)}) collective-permute-start(f32[2,2,2,64,512]{4,3,2,1,0:T(8,128)S(1)} %add_bitcast_fusion.6), channel_id=1, source_target_pairs={{0,2},{1,3},{2,0},{3,1},{4,6},{5,7},{6,4},{7,5},{8,10},{9,11},{10,... | collective-permute-start | bytes 3145736 | tf_op jit(solution)/shard_map/ppermute | solution.py:28
  251.9 49.1 %collective-permute-start.39 = (f32[2,2,2,64,512]{4,3,2,1,0:T(8,128)S(1)}, f32[2,2,2,64,512]{4,3,2,1,0:T(8,128)S(1)}, u32[]{:S(2)}, u32[]{:S(2)}) collective-permute-start(f32[2,2,2,64,512]{4,3,2,1,0:T(8,128)S(1)} %add_bitcast_fusion.5), channel_id=1, source_target_pairs={{0,8},{4,12},{8,0},{12,4},{16,24},{20,28},{24,16},{28,20},{1,9},{5... | collective-permute-start | bytes 3145736 | tf_op jit(solution)/shard_map/ppermute | solution.py:28
  255.4 48.6 %collective-permute-start.18 = (f32[2,2,2,64,512]{4,3,2,1,0:T(8,128)S(1)}, f32[2,2,2,64,512]{4,3,2,1,0:T(8,128)S(1)}, u32[]{:S(2)}, u32[]{:S(2)}) collective-permute-start(f32[2,2,2,64,512]{4,3,2,1,0:T(8,128)S(1)} %add_bitcast_fusion.8), channel_id=1, source_target_pairs={{0,4},{4,0},{8,12},{12,8},{16,20},{20,16},{24,28},{28,24},{1,5},{5... | collective-permute-start | bytes 3145736 | tf_op jit(solution)/shard_map/ppermute | solution.py:28
  255.5 40.0 %collective-permute-start.15 = (f32[2,11,128]{2,1,0:T(8,128)S(1)}, f32[2,11,128]{2,1,0:T(8,128)S(1)}, u32[]{:S(2)}, u32[]{:S(2)}) collective-permute-start(f32[2,11,128]{2,1,0:T(8,128)S(1)} %fusion.116), channel_id=1, source_target_pairs={{0,8},{4,12},{8,0},{12,4},{16,24},{20,28},{24,16},{28,20},{1,9},{5... | collective-permute-start | bytes 33800 | tf_op jit(solution)/shard_map/ppermute | solution.py:28
  295.5 26.1 %collective-permute-start.25 = (f32[2,2,2,64,512]{4,3,2,1,0:T(8,128)S(1)}, f32[2,2,2,64,512]{4,3,2,1,0:T(8,128)S(1)}, u32[]{:S(2)}, u32[]{:S(2)}) collective-permute-start(f32[2,2,2,64,512]{4,3,2,1,0:T(8,128)S(1)} %add_bitcast_fusion.7), channel_id=1, source_target_pairs={{0,2},{1,3},{2,0},{3,1},{4,6},{5,7},{6,4},{7,5},{8,10},{9,11},{10,... | collective-permute-start | bytes 3145736 | tf_op jit(solution)/shard_map/ppermute | solution.py:28
  298.7 36.5 %collective-permute-start.75 = (f32[2,2,64,512]{3,2,1,0:T(8,128)S(1)}, f32[2,2,64,512]{3,2,1,0:T(8,128)S(1)}, u32[]{:S(2)}, u32[]{:S(2)}) collective-permute-start(f32[2,2,64,512]{3,2,1,0:T(8,128)S(1)} %bitcast_add_fusion.4), channel_id=1, source_target_pairs={{0,16},{4,20},{8,24},{12,28},{16,0},{20,4},{24,8},{28,12},{1,17},{... | collective-permute-start | bytes 1572872 | tf_op jit(solution)/shard_map/ppermute | solution.py:28
  300.9 34.3 %collective-permute-start.33 = (f32[2,2,64,512]{3,2,1,0:T(8,128)S(1)}, f32[2,2,64,512]{3,2,1,0:T(8,128)S(1)}, u32[]{:S(2)}, u32[]{:S(2)}) collective-permute-start(f32[2,2,64,512]{3,2,1,0:T(8,128)S(1)} %bitcast_add_fusion.14), channel_id=1, source_target_pairs={{0,4},{4,0},{8,12},{12,8},{16,20},{20,16},{24,28},{28,24},{1,5},{5... | collective-permute-start | bytes 1572872 | tf_op jit(solution)/shard_map/ppermute | solution.py:28
  304.0 42.3 %collective-permute-start.40 = (f32[2,2,64,512]{3,2,1,0:T(8,128)S(1)}, f32[2,2,64,512]{3,2,1,0:T(8,128)S(1)}, u32[]{:S(2)}, u32[]{:S(2)}) collective-permute-start(f32[2,2,64,512]{3,2,1,0:T(8,128)S(1)} %bitcast_add_fusion.13), channel_id=1, source_target_pairs={{0,16},{4,20},{8,24},{12,28},{16,0},{20,4},{24,8},{28,12},{1,17},{... | collective-permute-start | bytes 1572872 | tf_op jit(solution)/shard_map/ppermute | solution.py:28
  307.3 42.7 %collective-permute-start.19 = (f32[2,2,64,512]{3,2,1,0:T(8,128)S(1)}, f32[2,2,64,512]{3,2,1,0:T(8,128)S(1)}, u32[]{:S(2)}, u32[]{:S(2)}) collective-permute-start(f32[2,2,64,512]{3,2,1,0:T(8,128)S(1)} %bitcast_add_fusion.16), channel_id=1, source_target_pairs={{0,2},{1,3},{2,0},{3,1},{4,6},{5,7},{6,4},{7,5},{8,10},{9,11},{10,... | collective-permute-start | bytes 1572872 | tf_op jit(solution)/shard_map/ppermute | solution.py:28
  321.6 108.8 %collective-permute-start.52 = (f32[1024,1024]{1,0:T(8,128)}, f32[1024,1024]{1,0:T(8,128)}, u32[]{:S(2)}, u32[]{:S(2)}) collective-permute-start(f32[1024,1024]{1,0:T(8,128)} %fusion.42), channel_id=1, source_target_pairs={{0,1},{1,0},{2,3},{3,2},{4,5},{5,4},{6,7},{7,6},{8,9},{9,8},{10,11... | collective-permute-start | bytes 12582920 | tf_op jit(solution)/shard_map/ppermute | solution.py:28
  335.2 98.8 %collective-permute-start.45 = (f32[1024,1024]{1,0:T(8,128)}, f32[1024,1024]{1,0:T(8,128)}, u32[]{:S(2)}, u32[]{:S(2)}) collective-permute-start(f32[1024,1024]{1,0:T(8,128)} %fusion.45), channel_id=1, source_target_pairs={{0,1},{1,0},{2,3},{3,2},{4,5},{5,4},{6,7},{7,6},{8,9},{9,8},{10,11... | collective-permute-start | bytes 12582920 | tf_op jit(solution)/shard_map/ppermute | solution.py:28
  335.2 101.5 %collective-permute-start.66 = (f32[4096,256]{1,0:T(8,128)S(1)}, f32[4096,256]{1,0:T(8,128)S(1)}, u32[]{:S(2)}, u32[]{:S(2)}) collective-permute-start(f32[4096,256]{1,0:T(8,128)S(1)} %copy-done.43), channel_id=1, source_target_pairs={{0,1},{1,0},{2,3},{3,2},{4,5},{5,4},{6,7},{7,6},{8,9},{9,8},{10,11... | collective-permute-start | bytes 12582920 | tf_op jit(solution)/shard_map/ppermute | solution.py:28
  350.0 88.6 %collective-permute-start.59 = (f32[4096,256]{1,0:T(8,128)S(1)}, f32[4096,256]{1,0:T(8,128)S(1)}, u32[]{:S(2)}, u32[]{:S(2)}) collective-permute-start(f32[4096,256]{1,0:T(8,128)S(1)} %copy-done.42), channel_id=1, source_target_pairs={{0,1},{1,0},{2,3},{3,2},{4,5},{5,4},{6,7},{7,6},{8,9},{9,8},{10,11... | collective-permute-start | bytes 12582920 | tf_op jit(solution)/shard_map/ppermute | solution.py:28
  438.6 95.0 %collective-permute-start.53 = (f32[2,2,2,64,1024]{4,3,2,1,0:T(8,128)S(1)}, f32[2,2,2,64,1024]{4,3,2,1,0:T(8,128)S(1)}, u32[]{:S(2)}, u32[]{:S(2)}) collective-permute-start(f32[2,2,2,64,1024]{4,3,2,1,0:T(8,128)S(1)} %add_bitcast_fusion.2), channel_id=1, source_target_pairs={{0,4},{4,0},{8,12},{12,8},{16,20},{20,16},{24,28},{28,24},{1,5},{5... | collective-permute-start | bytes 6291464 | tf_op jit(solution)/shard_map/ppermute | solution.py:28
  440.8 95.3 %collective-permute-start.46 = (f32[2,2,2,64,1024]{4,3,2,1,0:T(8,128)S(1)}, f32[2,2,2,64,1024]{4,3,2,1,0:T(8,128)S(1)}, u32[]{:S(2)}, u32[]{:S(2)}) collective-permute-start(f32[2,2,2,64,1024]{4,3,2,1,0:T(8,128)S(1)} %add_bitcast_fusion.3), channel_id=1, source_target_pairs={{0,2},{1,3},{2,0},{3,1},{4,6},{5,7},{6,4},{7,5},{8,10},{9,11},{10,... | collective-permute-start | bytes 6291464 | tf_op jit(solution)/shard_map/ppermute | solution.py:28
  441.6 97.6 %collective-permute-start.67 = (f32[2,2,2,256,256]{4,3,2,1,0:T(8,128)S(1)}, f32[2,2,2,256,256]{4,3,2,1,0:T(8,128)S(1)}, u32[]{:S(2)}, u32[]{:S(2)}) collective-permute-start(f32[2,2,2,256,256]{4,3,2,1,0:T(8,128)S(1)} %add_bitcast_fusion), channel_id=1, source_target_pairs={{0,4},{4,0},{8,12},{12,8},{16,20},{20,16},{24,28},{28,24},{1,5},{5... | collective-permute-start | bytes 6291464 | tf_op jit(solution)/shard_map/ppermute | solution.py:28
  444.1 96.5 %collective-permute-start.60 = (f32[2,2,2,256,256]{4,3,2,1,0:T(8,128)S(1)}, f32[2,2,2,256,256]{4,3,2,1,0:T(8,128)S(1)}, u32[]{:S(2)}, u32[]{:S(2)}) collective-permute-start(f32[2,2,2,256,256]{4,3,2,1,0:T(8,128)S(1)} %add_bitcast_fusion.1), channel_id=1, source_target_pairs={{0,2},{1,3},{2,0},{3,1},{4,6},{5,7},{6,4},{7,5},{8,10},{9,11},{10,... | collective-permute-start | bytes 6291464 | tf_op jit(solution)/shard_map/ppermute | solution.py:28
  445.7 83.1 %collective-permute-start.29 = (f32[64,512]{1,0:T(8,128)S(1)}, f32[64,512]{1,0:T(8,128)S(1)}, u32[]{:S(2)}, u32[]{:S(2)}) collective-permute-start(f32[64,512]{1,0:T(8,128)S(1)} %fusion.91), channel_id=1, source_target_pairs={{0,2},{1,3},{2,0},{3,1},{4,6},{5,7},{6,4},{7,5},{8,10},{9,11},{10,... | collective-permute-start | bytes 393224 | tf_op jit(solution)/shard_map/ppermute | solution.py:28
  535.1 26.1 %collective-permute-start.54 = (f32[2,2,64,1024]{3,2,1,0:T(8,128)S(1)}, f32[2,2,64,1024]{3,2,1,0:T(8,128)S(1)}, u32[]{:S(2)}, u32[]{:S(2)}) collective-permute-start(f32[2,2,64,1024]{3,2,1,0:T(8,128)S(1)} %bitcast_add_fusion.2), channel_id=1, source_target_pairs={{0,2},{1,3},{2,0},{3,1},{4,6},{5,7},{6,4},{7,5},{8,10},{9,11},{10,... | collective-permute-start | bytes 3145736 | tf_op jit(solution)/shard_map/ppermute | solution.py:28
  537.6 26.1 %collective-permute-start.47 = (f32[2,2,64,1024]{3,2,1,0:T(8,128)S(1)}, f32[2,2,64,1024]{3,2,1,0:T(8,128)S(1)}, u32[]{:S(2)}, u32[]{:S(2)}) collective-permute-start(f32[2,2,64,1024]{3,2,1,0:T(8,128)S(1)} %bitcast_add_fusion.3), channel_id=1, source_target_pairs={{0,4},{4,0},{8,12},{12,8},{16,20},{20,16},{24,28},{28,24},{1,5},{5... | collective-permute-start | bytes 3145736 | tf_op jit(solution)/shard_map/ppermute | solution.py:28
  539.4 43.7 %collective-permute-start.68 = (f32[2,2,256,256]{3,2,1,0:T(8,128)S(1)}, f32[2,2,256,256]{3,2,1,0:T(8,128)S(1)}, u32[]{:S(2)}, u32[]{:S(2)}) collective-permute-start(f32[2,2,256,256]{3,2,1,0:T(8,128)S(1)} %bitcast_add_fusion), channel_id=1, source_target_pairs={{0,2},{1,3},{2,0},{3,1},{4,6},{5,7},{6,4},{7,5},{8,10},{9,11},{10,... | collective-permute-start | bytes 3145736 | tf_op jit(solution)/shard_map/ppermute | solution.py:28
  540.8 44.4 %collective-permute-start.61 = (f32[2,2,256,256]{3,2,1,0:T(8,128)S(1)}, f32[2,2,256,256]{3,2,1,0:T(8,128)S(1)}, u32[]{:S(2)}, u32[]{:S(2)}) collective-permute-start(f32[2,2,256,256]{3,2,1,0:T(8,128)S(1)} %bitcast_add_fusion.1), channel_id=1, source_target_pairs={{0,4},{4,0},{8,12},{12,8},{16,20},{20,16},{24,28},{28,24},{1,5},{5... | collective-permute-start | bytes 3145736 | tf_op jit(solution)/shard_map/ppermute | solution.py:28
  583.2 26.7 %collective-permute-start.69 = (f32[2,256,256]{2,1,0:T(8,128)S(1)}, f32[2,256,256]{2,1,0:T(8,128)S(1)}, u32[]{:S(2)}, u32[]{:S(2)}) collective-permute-start(f32[2,256,256]{2,1,0:T(8,128)S(1)} %bitcast_add_fusion.5), channel_id=1, source_target_pairs={{0,8},{4,12},{8,0},{12,4},{16,24},{20,28},{24,16},{28,20},{1,9},{5... | collective-permute-start | bytes 1572872 | tf_op jit(solution)/shard_map/ppermute | solution.py:28
  585.4 34.9 %collective-permute-start.62 = (f32[2,256,256]{2,1,0:T(8,128)S(1)}, f32[2,256,256]{2,1,0:T(8,128)S(1)}, u32[]{:S(2)}, u32[]{:S(2)}) collective-permute-start(f32[2,256,256]{2,1,0:T(8,128)S(1)} %bitcast_add_fusion.7), channel_id=1, source_target_pairs={{0,8},{4,12},{8,0},{12,4},{16,24},{20,28},{24,16},{28,20},{1,9},{5... | collective-permute-start | bytes 1572872 | tf_op jit(solution)/shard_map/ppermute | solution.py:28
  588.2 32.3 %collective-permute-start.56 = (f32[64,1024]{1,0:T(8,128)S(1)}, f32[64,1024]{1,0:T(8,128)S(1)}, u32[]{:S(2)}, u32[]{:S(2)}) collective-permute-start(f32[64,1024]{1,0:T(8,128)S(1)} %bitcast_add_fusion.31), channel_id=1, source_target_pairs={{0,16},{4,20},{8,24},{12,28},{16,0},{20,4},{24,8},{28,12},{1,17},{... | collective-permute-start | bytes 786440 | tf_op jit(solution)/shard_map/ppermute | solution.py:28
  590.9 31.6 %collective-permute-start.49 = (f32[64,1024]{1,0:T(8,128)S(1)}, f32[64,1024]{1,0:T(8,128)S(1)}, u32[]{:S(2)}, u32[]{:S(2)}) collective-permute-start(f32[64,1024]{1,0:T(8,128)S(1)} %bitcast_add_fusion.37), channel_id=1, source_target_pairs={{0,16},{4,20},{8,24},{12,28},{16,0},{20,4},{24,8},{28,12},{1,17},{... | collective-permute-start | bytes 786440 | tf_op jit(solution)/shard_map/ppermute | solution.py:28
  610.1 26.9 %collective-permute-start.70 = (f32[256,256]{1,0:T(8,128)S(1)}, f32[256,256]{1,0:T(8,128)S(1)}, u32[]{:S(2)}, u32[]{:S(2)}) collective-permute-start(f32[256,256]{1,0:T(8,128)S(1)} %bitcast_add_fusion.19), channel_id=1, source_target_pairs={{0,16},{4,20},{8,24},{12,28},{16,0},{20,4},{24,8},{28,12},{1,17},{... | collective-permute-start | bytes 786440 | tf_op jit(solution)/shard_map/ppermute | solution.py:28
  (162 other events, 1643.9 us)
